TPU v7x, 128 devices: a whole 4x4x4 slice. The times are simulated.
128 devices in a mesh: grp: 4 (over x), seq: 32 (over z, y, core).
Axes of the slice: x: 4, y: 4, z: 4, core: 2. Of those that a mesh axis runs over, the one named last changes fastest.
Arguments:
- captions: bfloat16 [2048, 4096], P(('grp', 'seq')), may hold values from -6 to 6
- lengths: int32 [4, 8], replicated, may hold values from 1 to 300, 512 in all within a row
- clip_order: int32 [32], replicated, may hold values from 0 to 31, each once
- t5_gain: float32 [4096], replicated, may hold values from 0.5 to 1.5
- w_tq: bfloat16 [4096, 4096], P(None, 'seq'), may hold values from -0.13671875 to 0.13671875
- w_tk: bfloat16 [4096, 4096], P(None, 'seq'), may hold values from -0.09375 to 0.09375
- w_tv: bfloat16 [4096, 4096], P(None, 'seq'), may hold values from -0.09375 to 0.09375
- w_to: bfloat16 [4096, 4096], P('seq'), may hold values from -0.09375 to 0.09375
- w_kv: bfloat16 [4096, 2304], P(None, 'seq'), may hold values from -0.09375 to 0.09375
- video: bfloat16 [32, 2048, 1152], P('grp', 'seq'), may hold values from -6 to 6
- modulation: float32 [32, 3, 1152], P('grp'), may hold values from -4 to 4
- w_qkv: bfloat16 [1152, 3456], replicated, may hold values from -1.5320647 to 1.5320647
- w_o: bfloat16 [1152, 1152], replicated, may hold values from -0.1875 to 0.1875
- w_cq: bfloat16 [1152, 1152], replicated, may hold values from -2.0623948 to 2.0623948
- w_co: bfloat16 [1152, 1152], replicated, may hold values from -0.1875 to 0.1875
Outputs:
- video_out: bfloat16 [32, 2048, 1152], P('grp', 'seq')
Inputs may be any that keep to these rules, and one draw needn't show every extreme that they name: `lengths`: each row sums to 512, and the largest entry of each row is 300. `clip_order`: every clip is described by exactly one caption.
All inputs are finite; a program needn't handle non-finite values.
Results may differ from a plain program's by a relative error of at most 0.029.
The roundings to bfloat16 on the way count: a program that leaves them out, or rounds other values in their place, can miss the bound.
Values may be sent and summed in bfloat16 or wider, within the bound.
A program may use at most 320 MiB of HBM per device.

v0:
```python
import jax
import jax.numpy as jnp
from jax import lax
from jax.sharding import PartitionSpec as P

ET = 64
D = 1152
H = 16
E = 72
LMAX = 300


def rms_rows(rows, gain):
    values = rows.astype(jnp.float32)
    power = jnp.mean(values * values, axis=-1, keepdims=True)
    return (values * lax.rsqrt(power + 1e-06) * gain).astype(jnp.bfloat16)


def modulated_norm(rows, shift, scale):
    values = rows.astype(jnp.float32)
    center = values - jnp.mean(values, axis=-1, keepdims=True)
    spread = jnp.mean(center * center, axis=-1, keepdims=True)
    return (center * lax.rsqrt(spread + 1e-06) * (1.0 + scale) + shift).astype(jnp.bfloat16)


def masked_weights(score, keep):
    masked = jnp.where(keep, score, -1e30)
    highest = jnp.max(masked, axis=-1, keepdims=True)
    weight = jnp.where(keep, jnp.exp(masked - highest), 0.0)
    return (weight, jnp.sum(weight, axis=-1, keepdims=True))


def attend_items(block):
    item_count = block.shape[1]
    token_count = block.shape[2] // (3 * E)
    grid = block[0].reshape(item_count, token_count, 3, E)
    query_rows = min(512, token_count)

    def one_item(item):
        queries = item[:, 0]
        key_rows = item[:, 1]
        value_rows = item[:, 2]

        def one_block(query_block):
            score = lax.dot_general(
                query_block, key_rows, (((1,), (1,)), ((), ())), preferred_element_type=jnp.float32
            ) * E ** (-0.5)
            highest = jnp.max(score, axis=-1, keepdims=True)
            weight = jnp.exp(score - highest)
            total = jnp.sum(weight, axis=-1, keepdims=True)
            mixed = (
                jnp.dot(weight.astype(jnp.bfloat16), value_rows, preferred_element_type=jnp.float32)
                / total
            )
            return mixed.astype(jnp.bfloat16)

        blocks = lax.map(one_block, queries.reshape(token_count // query_rows, query_rows, E))
        return blocks.reshape(token_count * E)

    mixed_items = lax.map(one_item, grid)
    return mixed_items.reshape(1, item_count, token_count * E)


def per_device(
    captions,
    lengths,
    clip_order,
    t5_gain,
    w_tq,
    w_tk,
    w_tv,
    w_to,
    w_kv,
    video,
    modulation,
    w_qkv,
    w_o,
    w_cq,
    w_co,
):
    group = lax.axis_index("grp")
    seq_index = lax.axis_index("seq")
    seq_count = lax.axis_size("seq")
    own_rows = captions.shape[0]
    pack_rows = own_rows * seq_count
    local_width = w_tq.shape[1]
    head_local = local_width // ET
    stacked = jnp.concatenate([w_tq, w_tk, w_tv], axis=1)
    normed = rms_rows(lax.all_gather(captions, "seq", axis=0, tiled=True), t5_gain)
    projected = jnp.dot(normed, stacked, preferred_element_type=jnp.float32).astype(jnp.bfloat16)
    query = projected[:, :local_width].reshape(pack_rows, head_local, ET)
    key_rows = projected[:, local_width : 2 * local_width].reshape(pack_rows, head_local, ET)
    value_rows = projected[:, 2 * local_width :].reshape(pack_rows, head_local, ET)
    group_count = lengths.shape[0]
    chosen_group = jnp.arange(group_count, dtype=jnp.int32) == group
    pack_lengths = jnp.sum(jnp.where(chosen_group[:, None], lengths, 0), axis=0)
    ends = jnp.cumsum(pack_lengths)
    position = jnp.arange(pack_rows, dtype=jnp.int32)
    segment = jnp.sum((position[:, None] >= ends[None, :]).astype(jnp.int32), axis=1)
    same = (segment[:, None] == segment[None, :])[None]
    score = jnp.einsum("qhe,khe->hqk", query, key_rows, preferred_element_type=jnp.float32)
    weight, total = masked_weights(score, same)
    mixed = (
        jnp.einsum(
            "hqk,khe->hqe",
            weight.astype(jnp.bfloat16),
            value_rows,
            preferred_element_type=jnp.float32,
        )
        / total
    )
    mixed = mixed.astype(jnp.bfloat16)
    partial_value = jnp.einsum(
        "hqe,hed->qd",
        mixed,
        w_to.reshape(head_local, ET, w_to.shape[1]),
        preferred_element_type=jnp.float32,
    )
    first_row = seq_index * own_rows
    own_part = lax.dynamic_slice_in_dim(partial_value, first_row, own_rows, 0) + captions.astype(
        jnp.float32
    )
    partial_value = lax.dynamic_update_slice_in_dim(partial_value, own_part, first_row, 0)
    encoded = lax.psum(partial_value, "seq").astype(jnp.bfloat16)
    columns = lax.dot_general(
        w_kv, encoded, (((0,), (1,)), ((), ())), preferred_element_type=jnp.float32
    ).astype(jnp.bfloat16)
    context = lax.all_gather(columns, ("grp", "seq"), axis=0, tiled=True)
    context = context.reshape(-1, 2 * D, pack_rows)
    clips_local = video.shape[0]
    tokens_local = video.shape[1]
    shift = modulation[:, 0][:, None, :]
    scale = modulation[:, 1][:, None, :]
    gate = modulation[:, 2][:, None, :]
    video_norm = modulated_norm(video, shift, scale)
    video_proj = jnp.einsum(
        "ctd,dshe->chtse", video_norm, w_qkv.reshape(D, 3, H, E), preferred_element_type=jnp.float32
    ).astype(jnp.bfloat16)
    outgoing = video_proj.reshape(seq_count, -1, tokens_local * 3 * E)
    mixed_heads = attend_items(
        lax.all_to_all(outgoing, "seq", split_axis=0, concat_axis=2, tiled=True)
    )
    returned = lax.all_to_all(mixed_heads, "seq", split_axis=2, concat_axis=0, tiled=True)
    returned = returned.reshape(clips_local, H, tokens_local, E)
    attended = jnp.einsum(
        "chte,hed->ctd", returned, w_o.reshape(H, E, D), preferred_element_type=jnp.float32
    )
    hidden = (video.astype(jnp.float32) + gate * attended).astype(jnp.bfloat16)
    clip_count = clip_order.shape[0]
    all_ids = jnp.arange(clip_count, dtype=jnp.int32)
    clip_ids = group * clips_local + jnp.arange(clips_local, dtype=jnp.int32)
    match = clip_order[None, :] == clip_ids[:, None]
    caption = jnp.sum(jnp.where(match, all_ids[None, :], 0), axis=1)
    flat_length = lengths.reshape(-1)
    flat_end = jnp.cumsum(lengths, axis=1).reshape(-1)
    onehot = caption[:, None] == all_ids[None, :]
    cap_length = jnp.sum(jnp.where(onehot, flat_length[None, :], 0), axis=1)
    cap_start = jnp.sum(jnp.where(onehot, flat_end[None, :], 0), axis=1) - cap_length
    source = caption // clips_local
    slot = jnp.minimum(
        cap_start[:, None] + jnp.arange(LMAX, dtype=jnp.int32)[None, :], pack_rows - 1
    )
    picked = context[source[:, None], :, slot]
    cross_key = picked[:, :, :D].reshape(clips_local, LMAX, H, E)
    cross_value = picked[:, :, D:].reshape(clips_local, LMAX, H, E)
    cross_query = jnp.dot(hidden.reshape(-1, D), w_cq, preferred_element_type=jnp.float32).astype(
        jnp.bfloat16
    )
    cross_query = cross_query.reshape(clips_local, tokens_local, H, E)
    cross_score = jnp.einsum(
        "cthe,cphe->chtp", cross_query, cross_key, preferred_element_type=jnp.float32
    ) * E ** (-0.5)
    keep = (jnp.arange(LMAX, dtype=jnp.int32)[None, :] < cap_length[:, None])[:, None, None, :]
    cross_weight, cross_total = masked_weights(cross_score, keep)
    cross_mix = jnp.einsum(
        "chtp,cphe->cthe",
        cross_weight.astype(jnp.bfloat16),
        cross_value,
        preferred_element_type=jnp.float32,
    )
    cross_mix = (cross_mix / jnp.transpose(cross_total, (0, 2, 1, 3))).astype(jnp.bfloat16)
    update = jnp.dot(cross_mix.reshape(-1, D), w_co, preferred_element_type=jnp.float32)
    result = hidden.astype(jnp.float32) + update.reshape(clips_local, tokens_local, D)
    return result.astype(jnp.bfloat16)


def solution(mesh):
    in_specs = (
        P(("grp", "seq"), None),
        P(),
        P(),
        P(),
        P(None, "seq"),
        P(None, "seq"),
        P(None, "seq"),
        P("seq", None),
        P(None, "seq"),
        P("grp", "seq", None),
        P("grp", None, None),
        P(),
        P(),
        P(),
        P(),
    )
    out_specs = P("grp", "seq", None)
    return jax.shard_map(
        per_device, mesh=mesh, in_specs=in_specs, out_specs=out_specs, check_vma=False
    )
```

profile of v0, /device:TPU:2, one launch (start us, length us, event | category | flops | bytes accessed | tf_op | source)
XLA Modules:
  0.0 1338.9 jit_solution(8260195939617497902)
XLA Ops:
  7.3 11.6 copy.62
  22.8 12.7 convert_bitcast_fusion
  35.5 18.9 %copy.63 = bf16[8,16,64,3,72]{4,3,2,1,0:T(4,128)(2,1)} copy(bf16[8,16,64,3,72]{4,2,1,3,0:T(8,128)(2,1)} %convert_bitcast_fusion) | data formatting | bytes 7077888 | tf_op jit(solution)/shard_map/convert_element_type | solution.py:138
  54.4 15.8 %reshape.230 = bf16[32,4,13824]{2,1,0:T(4,128)(2,1)} reshape(bf16[8,16,64,3,72]{4,3,2,1,0:T(4,128)(2,1)} %copy.63) | data formatting | bytes 7077888 | tf_op jit(solution)/shard_map/reshape | solution.py:139
  70.2 8.6 all-to-all-start
  79.4 45.5 %all-to-all-done = bf16[32,4,13824]{2,1,0:T(4,128)(2,1)} async-done(((bf16[32,4,13824]{2,1,0:T(4,128)(2,1)}), bf16[32,4,13824]{2,1,0:T(4,128)(2,1)}, u32[]{:S(2)}, u32[]{:S(2)}) %all-to-all-start) | async-done | bytes 3538976 | tf_op jit(solution)/shard_map/all_to_all | solution.py:141
  129.4 17.2 %reshape_squeeze.3 = bf16[4,2048,3,72]{3,2,1,0:T(4,128)(2,1)} reshape(bf16[1,4,32,13824]{3,2,1,0:T(8,128)(2,1)} %copy.64) | data formatting | bytes 7077888 | tf_op jit(solution)/shard_map/reshape;squeeze | solution.py:36
  146.6 7.4 copy.65
  171.6 154.0 %all-reduce.1 = bf16[512,4096]{1,0:T(8,128)(2,1)} all-reduce(f32[512,4096]{1,0:T(8,128)} %add_dynamic-update-slice_fusion), channel_id=1, replica_groups=mesh['grp'=4,'seq'=32] {'seq'}, use_global_device_ids=true, to_apply=%region_14.15 | all-reduce | flops 2097152 | bytes 12582912 | tf_op jit(solution)/shard_map/psum | solution.py:124
  329.8 125.6 %while.21 = (s32[]{:T(128)}, bf16[4,147456]{1,0:T(4,128)(2,1)}, bf16[4,2048,3,72]{3,1,2,0:T(8,128)(2,1)}, s32[]{:T(128)}, s32[]{:T(128)}, /*index=5*/s32[]{:T(128)}) while((s32[]{:T(128)}, bf16[4,147456]{1,0:T(4,128)(2,1)}, bf16[4,2048,3,72]{3,1,2,0:T(8,128)(2,1)}, s32[]{:T(128)}, s32[]{:T(128)}, /*index=5*/s32[]{:T(128)}) %tuple.58), condition=%wide.region_7.8_spmd, body=%wide.region_2.7_spmd.sunk | while | flops 310451200 | bytes 19155660 | solution.py:60
  332.4 14.9 %while.22 = (s32[]{:T(128)}, bf16[4,512,72]{1,2,0:T(8,128)(2,1)S(1)}, bf16[4,512,72]{2,1,0:T(8,128)(2,1)}, bf16[2048,72]{1,0:T(8,128)(2,1)}, bf16[2048,72]{1,0:T(8,128)(2,1)S(1)}, /*index=5*/s32[]{:T(128)}) while((s32[]{:T(128)}, bf16[4,512,72]{1,2,0:T(8,128)(2,1)S(1)}, bf16[4,512,72]{2,1,0:T(8,128)(2,1)}, bf16[2048,72]{1,0:T(8,128)(2,1)}, ...), condition=%wide.region_6.6_spmd, body=%wide.region_3.5_spmd.sunk | while | flops 310451200 | bytes 13847113 | solution.py:57
  350.4 10.8 dynamic_update_slice.16
  363.8 14.9 %while.22 = (s32[]{:T(128)}, bf16[4,512,72]{1,2,0:T(8,128)(2,1)S(1)}, bf16[4,512,72]{2,1,0:T(8,128)(2,1)}, bf16[2048,72]{1,0:T(8,128)(2,1)}, bf16[2048,72]{1,0:T(8,128)(2,1)S(1)}, /*index=5*/s32[]{:T(128)}) while((s32[]{:T(128)}, bf16[4,512,72]{1,2,0:T(8,128)(2,1)S(1)}, bf16[4,512,72]{2,1,0:T(8,128)(2,1)}, bf16[2048,72]{1,0:T(8,128)(2,1)}, ...), condition=%wide.region_6.6_spmd, body=%wide.region_3.5_spmd.sunk | while | flops 310451200 | bytes 13847113 | solution.py:57
  381.8 10.9 dynamic_update_slice.16
  395.3 14.9 %while.22 = (s32[]{:T(128)}, bf16[4,512,72]{1,2,0:T(8,128)(2,1)S(1)}, bf16[4,512,72]{2,1,0:T(8,128)(2,1)}, bf16[2048,72]{1,0:T(8,128)(2,1)}, bf16[2048,72]{1,0:T(8,128)(2,1)S(1)}, /*index=5*/s32[]{:T(128)}) while((s32[]{:T(128)}, bf16[4,512,72]{1,2,0:T(8,128)(2,1)S(1)}, bf16[4,512,72]{2,1,0:T(8,128)(2,1)}, bf16[2048,72]{1,0:T(8,128)(2,1)}, ...), condition=%wide.region_6.6_spmd, body=%wide.region_3.5_spmd.sunk | while | flops 310451200 | bytes 13847113 | solution.py:57
  413.2 10.8 dynamic_update_slice.16
  426.6 14.9 %while.22 = (s32[]{:T(128)}, bf16[4,512,72]{1,2,0:T(8,128)(2,1)S(1)}, bf16[4,512,72]{2,1,0:T(8,128)(2,1)}, bf16[2048,72]{1,0:T(8,128)(2,1)}, bf16[2048,72]{1,0:T(8,128)(2,1)S(1)}, /*index=5*/s32[]{:T(128)}) while((s32[]{:T(128)}, bf16[4,512,72]{1,2,0:T(8,128)(2,1)S(1)}, bf16[4,512,72]{2,1,0:T(8,128)(2,1)}, bf16[2048,72]{1,0:T(8,128)(2,1)}, ...), condition=%wide.region_6.6_spmd, body=%wide.region_3.5_spmd.sunk | while | flops 310451200 | bytes 13847113 | solution.py:57
  444.6 10.8 dynamic_update_slice.16
  455.4 128.5 %copy.66 = bf16[1,4,147456]{1,0,2:T(2,128)(2,1)} copy(bf16[1,4,147456]{2,1,0:T(4,128)(2,1)} %bitcast.133) | data formatting | bytes 2359296 | tf_op jit(solution)/shard_map/reshape | solution.py:61
  584.4 225.6 %reduce = bf16[147456,4]{1,0:T(8,128)(2,1)} reduce(bf16[147456,1,4]{2,1,0:T(2,128)(2,1)} %bitcast.87, bf16[]{:T(256)} %broadcast.220), dimensions={1}, to_apply=%bitcast.87.reduce_sub_computation | reduce | bytes 2359298
  810.1 69.3 %reshape.257 = bf16[32,2,9216]{2,1,0:T(2,128)(2,1)} reshape(bf16[147456,4]{1,0:T(8,128)(2,1)} %reduce) | data formatting | bytes 2359296
  885.2 18.0 %all-to-all-done.1 = bf16[32,2,9216]{2,1,0:T(2,128)(2,1)} async-done(((bf16[32,2,9216]{2,1,0:T(2,128)(2,1)}), bf16[32,2,9216]{2,1,0:T(2,128)(2,1)}, u32[]{:S(2)}, u32[]{:S(2)}) %all-to-all-start.1) | async-done | bytes 1179680 | tf_op jit(solution)/shard_map/all_to_all | solution.py:143
  903.2 87.5 %reshape.258 = bf16[147456,1,4]{2,1,0:T(2,128)(2,1)} reshape(bf16[32,2,9216]{2,1,0:T(2,128)(2,1)} %all-to-all-done.1) | data formatting | bytes 2359296
  990.7 136.9 %copy.67 = bf16[1,4,147456]{2,1,0:T(4,128)(2,1)} copy(bf16[1,4,147456]{1,0,2:T(2,128)(2,1)} %bitcast.88) | data formatting | bytes 2359296 | tf_op jit(solution)/shard_map/all_to_all | solution.py:143
  1151.3 12.1 copy.70
  1163.4 96.4 %gather_fusion = bf16[2400,2304]{1,0:T(8,128)(2,1)} fusion(bf16[4,2304,512]{1,2,0:T(8,128)(2,1)} %copy.70, s32[2400]{0:T(1024)S(1)} %reshape.245), kind=kCustom, calls=%fused_computation | custom fusion | bytes 22137600 | tf_op jit(solution)/shard_map/gather | solution.py:163
  1259.8 9.2 reshape.248
  1269.0 9.2 fusion.95
  1278.2 9.2 copy.72
  1287.4 9.2 copy.71
  1302.1 7.7 fusion.98
  1309.8 9.3 fusion.36
  (141 shorter events, 161.3 us)
Async XLA Ops:
  6.5 1131.1 %copy-start = (bf16[1152,1152]{1,0:T(8,128)(2,1)S(1)}, bf16[1152,1152]{1,0:T(8,128)(2,1)}, u32[]{:S(2)}) copy-start(bf16[1152,1152]{1,0:T(8,128)(2,1)} %param.31) | copy-start | bytes 7962628
  6.5 147.5 %all-gather.3.cloned.1.call-start = ((), (), s32[]{:S(2)}) async-start(), calls=%async_computation.2 | async-start | bytes 4325376 | tf_op jit(solution)/shard_map/all_gather | solution.py:89
  7.3 14.9 %copy-start.4 = (f32[8,3,1152]{2,0,1:T(8,128)S(1)}, f32[8,3,1152]{2,0,1:T(8,128)}, u32[]{:S(2)}) copy-start(f32[8,3,1152]{2,0,1:T(8,128)} %param.29) | copy-start | bytes 331780
  70.2 8.7 copy-start.6
  70.2 54.8 %all-to-all-start = ((bf16[32,4,13824]{2,1,0:T(4,128)(2,1)}), bf16[32,4,13824]{2,1,0:T(4,128)(2,1)}, u32[]{:S(2)}, u32[]{:S(2)}) async-start(bf16[32,4,13824]{2,1,0:T(4,128)(2,1)} %reshape.230), calls=%async_computation | async-start | bytes 7077888 | tf_op jit(solution)/shard_map/all_to_all | solution.py:141
  78.7 1072.6 %all-gather.5.cloned.1.call-start = ((), (), s32[]{:S(2)}) async-start(), calls=%async_computation.3 | async-start | bytes 9510912 | tf_op jit(solution)/shard_map/all_gather | solution.py:128
  146.6 10.7 copy-start.9
  154.0 3.4 copy-start.1
  163.6 6.4 copy-start.3
  171.6 154.0 %copy-start.2 = (bf16[4096,72]{0,1:T(8,128)(2,1)S(1)}, bf16[4096,72]{0,1:T(8,128)(2,1)}, u32[]{:S(2)}) copy-start(bf16[4096,72]{0,1:T(8,128)(2,1)} %param.27) | copy-start | bytes 1769476
  810.1 74.1 %copy-start.7 = (s32[4,8]{1,0:T(4,128)S(1)}, s32[4,8]{1,0:T(4,128)}, u32[]{:S(2)}) copy-start(s32[4,8]{1,0:T(4,128)} %param.20) | copy-start | bytes 388
  810.1 74.5 %copy-start.10 = (s32[32]{0:T(128)S(1)}, s32[32]{0:T(128)}, u32[]{:S(2)}) copy-start(s32[32]{0:T(128)} %param.21) | copy-start | bytes 388
  879.3 23.9 %all-to-all-start.1 = ((bf16[32,2,9216]{2,1,0:T(2,128)(2,1)}), bf16[32,2,9216]{2,1,0:T(2,128)(2,1)}, u32[]{:S(2)}, u32[]{:S(2)}) async-start(bf16[32,2,9216]{2,1,0:T(2,128)(2,1)} %reshape.257), calls=%async_computation.1 | async-start | bytes 2359296 | tf_op jit(solution)/shard_map/all_to_all | solution.py:143
  1129.1 8.5 copy-start.5
  1137.6 5.1 copy-start.8
  1141.7 1.0 copy-start.11
Sparse Core Ops, SparseCore 0:
  9.6 48.7 all-gather.2
  329.9 66.3 all-gather.4
where the time goes:
time: 1360 us; the launch traced here: 1340 us
  local copies, waits for them, and re-layouts  734 us (54%)
  other arithmetic  257 us (19%)
  blocking collectives  154 us (11%)
  matrix products  103 us (8%)
  waiting for transfers between devices  64.3 us (5%)
  between operations  13.9 us (1%)
    unnamed x1, other arithmetic  226 us
    unnamed x29, local copies, waits for them, and re-layouts  172 us
    psum x1, blocking collectives, per_device(): encoded = lax.psum(partial_value, 'seq').astype(jnp.bfloat16)  154 us
    all_to_all x2, local copies, waits for them, and re-layouts, per_device(): lax.all_to_all(mixed_heads, 'seq', split_axis=2, concat_axis=0, tiled=True)  139 us
    reshape x1, local copies, waits for them, and re-layouts, attend_items(): return mixed_items.reshape(1, item_count, token_count * E)  129 us
    gather x2, local copies, waits for them, and re-layouts, per_device(): picked = context[source[:, None], :, slot]  106 us
    all_to_all x1, waiting for transfers between devices, per_device(): lax.all_to_all(outgoing, 'seq', split_axis=0, concat_axis=2, tiled=True)  45.5 us
    dynamic_update_slice x4, local copies, waits for them, and re-layouts, attend_items(): mixed_items = lax.map(one_item, grid)  43.4 us
  transfers between devices with their start and end apart: 4, of which 2 were waited for; matrix products, arithmetic and copies ran while one was open for 66% of the time, Pallas kernels for 0%

commit v1 on v0

v1 whole, which is shorter than its diff:
```python
import functools
import math

import jax
import jax.numpy as jnp
from jax import lax
from jax.experimental import pallas as pl
from jax.experimental.pallas import tpu as pltpu
from jax.sharding import PartitionSpec as P

ET = 64
D = 1152
H = 16
E = 72
DT = 4096
HALF = DT // 2
LANE = 128
WIN = 384
HP = 4 * LANE
KEYS = 512
EP = 80
VT = 2048
MIB = 1024 * 1024
LOG2E = math.log2(math.e)
QSCALE = E ** (-0.5) * LOG2E
BF = jnp.bfloat16
F32 = jnp.float32
MESH = pl.DeviceIdType.MESH


def place():
    seq = lax.axis_index("seq")
    core = seq % 2
    chip = seq // 2
    return seq, core, chip, chip % 4, chip // 4


def remote(src, dst, send, recv, peer, axis="seq"):
    return pltpu.make_async_remote_copy(
        src_ref=src,
        dst_ref=dst,
        send_sem=send,
        recv_sem=recv,
        device_id={axis: peer},
        device_id_type=MESH,
    )


def greet(peer, axis="seq"):
    pl.semaphore_signal(
        pltpu.get_barrier_semaphore(), inc=1, device_id={axis: peer}, device_id_type=MESH
    )


def head_select(offset):
    row = lax.broadcasted_iota(jnp.int32, (WIN, HP), 0)
    col = lax.broadcasted_iota(jnp.int32, (WIN, HP), 1)
    head = col >> 7
    lane = col & 127
    hit = (row == offset + head * E + lane) & (lane < E)
    return jnp.where(hit, 1.0, 0.0).astype(BF)


def head_merge(offset):
    row = lax.broadcasted_iota(jnp.int32, (HP, WIN), 0)
    col = lax.broadcasted_iota(jnp.int32, (HP, WIN), 1)
    head = row >> 7
    lane = row & 127
    hit = (col == offset + head * E + lane) & (lane < E)
    return jnp.where(hit, 1.0, 0.0).astype(BF)


class Gather:
    def __init__(self, buf, send, recv):
        seq, core, chip, y, z = place()
        sib = seq + 1 - 2 * core
        first = buf.at[z, y, core, :, pl.ds(0, HALF)]
        second = buf.at[z, y, core, :, pl.ds(HALF, HALF)]
        row = buf.at[z, :, core, :, pl.ds(0, HALF)]
        col = buf.at[:, y, core, :, pl.ds(HALF, HALF)]
        self.a, self.b = [], []
        for j in range(1, 4):
            py = 8 * z + 2 * ((y + j) % 4) + core
            pz = 8 * ((z + j) % 4) + 2 * y + core
            n = j - 1
            self.a.append(remote(first, first, send.at[n], recv.at[n], py))
            self.a.append(remote(second, second, send.at[n + 3], recv.at[n + 3], pz))
            self.b.append(remote(row, row, send.at[n + 6], recv.at[n + 6], pz))
            self.b.append(remote(col, col, send.at[n + 9], recv.at[n + 9], py))
        half = buf.at[:, :, core]
        self.c = remote(half, half, send.at[12], recv.at[12], sib)

    def start(self):
        for copy in self.a:
            copy.start()

    def middle(self):
        for copy in self.a:
            copy.wait_recv()
        for copy in self.b:
            copy.start()

    def last(self):
        for copy in self.b:
            copy.wait_recv()
        self.c.start()

    def finish(self):
        self.c.wait_recv()
        for copy in self.a + self.b + [self.c]:
            copy.wait_send()


def front_kernel(
    lengths,
    gain,
    cap_in,
    mod,
    video,
    wq,
    wk,
    wv,
    wto_in,
    wqkv,
    heads_out,
    quarter_out,
    enc_out,
    cap,
    wt,
    wto,
    wwin,
    wpad,
    vid,
    tacc,
    mixb,
    s1,
    r1,
    acc,
    s2,
    r2,
    part,
    s3,
    r3,
    w_sem,
    ag_send,
    ag_recv,
    v_send,
    v_recv,
    f_send,
    f_recv,
    r_send,
    r_recv,
    o_sem,
):
    seq, core, chip, y, z = place()
    grp = lax.axis_index("grp")
    sib = seq + 1 - 2 * core
    quarter = seq % 4
    clip = seq // 4
    barrier = pltpu.get_barrier_semaphore()
    greet(sib)

    def greet_one(i, carry):
        greet(2 * ((chip + i) % 16) + core)
        return carry

    lax.fori_loop(1, 16, greet_one, 0)

    loads = [
        pltpu.make_async_copy(wq, wt.at[:, pl.ds(0, 128)], w_sem.at[0]),
        pltpu.make_async_copy(wk, wt.at[:, pl.ds(128, 128)], w_sem.at[1]),
        pltpu.make_async_copy(wv, wt.at[:, pl.ds(256, 128)], w_sem.at[2]),
        pltpu.make_async_copy(wto_in, wto, w_sem.at[3]),
    ]
    base = pl.multiple_of(256 * quarter, 128)
    for n in range(3):
        loads.append(
            pltpu.make_async_copy(
                wqkv.at[:, pl.ds(n * D + base, WIN)], wwin.at[n], w_sem.at[4 + n]
            )
        )
    own_video = pltpu.make_async_copy(video.at[clip], vid.at[seq], w_sem.at[7])
    for copy in loads:
        copy.start()
    own_video.start()

    rows = cap_in[...].astype(F32)
    power = jnp.mean(rows * rows, axis=-1, keepdims=True)
    cap[z, y, core] = (rows * lax.rsqrt(power + 1e-06) * gain[...]).astype(BF)

    pl.semaphore_wait(barrier, 16)
    gather = Gather(cap, ag_send, ag_recv)
    gather.start()

    for copy in loads[4:]:
        copy.wait()
    select = head_select(32 * quarter)
    for n in range(3):
        wpad[:, n * HP : (n + 1) * HP] = jnp.dot(
            wwin[n], select, preferred_element_type=F32
        ).astype(BF)
    gather.middle()

    def send_video(i):
        to = (chip + i) % 16
        return remote(video.at[to // 2], vid.at[seq], v_send.at[i], v_recv.at[i], 2 * to + core)

    def start_video(i, carry):
        send_video(i).start()
        return carry

    lax.fori_loop(1, 16, start_video, 0)
    for copy in loads[:4]:
        copy.wait()
    own_video.wait()
    gather.last()

    row_pos = lax.broadcasted_iota(jnp.int32, (KEYS, KEYS), 0)
    col_pos = lax.broadcasted_iota(jnp.int32, (KEYS, KEYS), 1)
    row_seg = jnp.zeros((KEYS, KEYS), jnp.int32)
    col_seg = jnp.zeros((KEYS, KEYS), jnp.int32)
    end = jnp.int32(0)
    for n in range(8):
        end = end + lengths[grp, n]
        row_seg = row_seg + (row_pos >= end).astype(jnp.int32)
        col_seg = col_seg + (col_pos >= end).astype(jnp.int32)
    same = row_seg == col_seg

    gather.finish()
    tacc[...] = jnp.zeros_like(tacc)

    def project(n, carry):
        at = pl.multiple_of(n * 512, 512)
        left = cap[:, :, :, :, pl.ds(at, 512)].reshape(KEYS, 512)
        tacc[...] += jnp.dot(left, wt[pl.ds(at, 512), :], preferred_element_type=F32)
        return carry

    lax.fori_loop(0, 8, project, 0)
    tquery = tacc[:, 0:128].astype(BF)
    tkey = tacc[:, 128:256].astype(BF)
    tvalue = tacc[:, 256:384].astype(BF)
    lane = lax.broadcasted_iota(jnp.int32, (KEYS, LANE), 1)
    mixes = []
    for n in range(2):
        own = (lane >= n * ET) & (lane < (n + 1) * ET)
        head_query = jnp.where(own, tquery.astype(F32), 0.0).astype(BF)
        score = lax.dot_general(
            head_query, tkey, (((1,), (1,)), ((), ())), preferred_element_type=F32
        )
        score = jnp.where(same, score, -1e30)
        weight = jnp.exp(score - jnp.max(score, axis=-1, keepdims=True))
        total = jnp.sum(weight, axis=-1, keepdims=True)
        mixes.append(jnp.dot(weight.astype(BF), tvalue, preferred_element_type=F32) / total)
    mixed = jnp.where(lane < ET, mixes[0], mixes[1]).astype(BF)
    mixb[...] = mixed.reshape(4, 4, 2, 16, LANE)

    def partial_rows(which, out):
        left = mixb[:, :, which].reshape(256, LANE)

        def one(n, carry):
            at = pl.multiple_of(n * 512, 512)
            value = jnp.dot(left, wto[:, pl.ds(at, 512)], preferred_element_type=F32)
            out[:, :, :, pl.ds(at, 512)] = value.reshape(4, 4, 16, 512).astype(out.dtype)
            return carry

        lax.fori_loop(0, 8, one, 0)

    partial_rows(1 - core, s1)
    pair = remote(s1, r1, r_send.at[0], r_recv.at[0], sib)
    pair.start()
    partial_rows(core, acc)
    pair.wait_recv()

    def add_pair(n, carry):
        at = pl.multiple_of(n * 512, 512)
        value = acc[:, :, :, pl.ds(at, 512)] + r1[:, :, :, pl.ds(at, 512)].astype(F32)
        acc[:, :, :, pl.ds(at, 512)] = value
        s2[:, :, :, pl.ds(at, 512)] = value.astype(BF)
        return carry

    lax.fori_loop(0, 8, add_pair, 0)
    second = []
    for j in range(1, 4):
        ty = (y + j) % 4
        tz = (z + j) % 4
        second.append(
            remote(
                s2.at[:, ty, :, pl.ds(0, HALF)],
                r2.at[0, j - 1],
                r_send.at[j],
                r_recv.at[j],
                8 * z + 2 * ty + core,
            )
        )
        second.append(
            remote(
                s2.at[tz, :, :, pl.ds(HALF, HALF)],
                r2.at[1, j - 1],
                r_send.at[3 + j],
                r_recv.at[3 + j],
                8 * tz + 2 * y + core,
            )
        )
    for copy in second:
        copy.start()

    shift = mod[clip, 0:1, :]
    scale = 1.0 + mod[clip, 1:2, :]
    vlane = lax.broadcasted_iota(jnp.int32, (256, HP), 1) & 127

    def forward(i):
        slot = 2 * ((chip + 16 - i) % 16) + core
        return remote(vid.at[slot], vid.at[slot], f_send.at[i], f_recv.at[i], sib)

    def arrive(i):
        send_video(i).wait_recv()
        forward(i).start()

    def norm(at):
        values = vid[pl.ds(2 * at, 2)].reshape(128, D).astype(F32)
        center = values - jnp.mean(values, axis=-1, keepdims=True)
        spread = jnp.mean(center * center, axis=-1, keepdims=True)
        return (center * lax.rsqrt(spread + 1e-06) * scale + shift).astype(BF)

    forward(0).start()
    arrive(1)

    def project_video(n, carry):
        @pl.when(n < 7)
        def _():
            arrive(2 * n + 2)
            arrive(2 * n + 3)

        forward(2 * n).wait_recv()
        forward(2 * n + 1).wait_recv()
        at0 = (chip + 16 - 2 * n) % 16
        at1 = (chip + 15 - 2 * n) % 16
        normed = jnp.concatenate([norm(at0), norm(at1)], axis=0)
        for which in range(3):
            value = jnp.dot(
                normed, wpad[:, which * HP : (which + 1) * HP], preferred_element_type=F32
            )
            if which == 0:
                value = value * QSCALE
            if which == 2:
                value = jnp.where(vlane == E, 1.0, value)
            value = value.astype(BF)
            for h in range(4):
                piece = value[:, h * LANE : (h + 1) * LANE]
                heads_out[which, h, at0] = piece[:128]
                heads_out[which, h, at1] = piece[128:]
        return carry

    lax.fori_loop(0, 8, project_video, 0)
    keep = pltpu.make_async_copy(vid.at[pl.ds(8 * quarter, 8)], quarter_out, o_sem)
    keep.start()

    for copy in second:
        copy.wait_recv()
    for n in range(4):
        first = acc[n, y, :, 0:HALF]
        other = acc[z, n, :, HALF:DT]
        for j in range(3):
            first = first + r2[0, j, n].astype(F32)
            other = other + r2[1, j, n].astype(F32)
        part[0, n] = first
        part[1, n] = other
        s3[0, n] = first.astype(BF)
        s3[1, n] = other.astype(BF)
    third = []
    for j in range(1, 4):
        ty = (y + j) % 4
        tz = (z + j) % 4
        third.append(
            remote(
                s3.at[0, tz],
                r3.at[0, j - 1],
                r_send.at[6 + j],
                r_recv.at[6 + j],
                8 * tz + 2 * y + core,
            )
        )
        third.append(
            remote(
                s3.at[1, ty],
                r3.at[1, j - 1],
                r_send.at[9 + j],
                r_recv.at[9 + j],
                8 * z + 2 * ty + core,
            )
        )
    for copy in third:
        copy.start()
    for copy in third:
        copy.wait_recv()
    first = part[0, z]
    other = part[1, y]
    for j in range(3):
        first = first + r3[0, j].astype(F32)
        other = other + r3[1, j].astype(F32)
    enc_out[:, 0:HALF] = (cap_in[:, 0:HALF].astype(F32) + first).astype(BF)
    enc_out[:, HALF:DT] = (cap_in[:, HALF:DT].astype(F32) + other).astype(BF)

    keep.wait()
    pair.wait_send()
    for copy in second + third:
        copy.wait_send()

    def drain(i, carry):
        send_video(i).wait_send()
        forward(i).wait_send()
        return carry

    lax.fori_loop(1, 16, drain, 0)
    forward(0).wait_send()


def attend_kernel(
    clip_order,
    enc_in,
    wkv,
    heads,
    win_out,
    kv_out,
    enc,
    mix,
    merge,
    outw,
    ctxf,
    ctx4,
    sel,
    ag_send,
    ag_recv,
    x_send,
    x_recv,
    c_send,
    c_recv,
    p_send,
    p_recv,
    q_send,
    q_recv,
):
    seq, core, chip, y, z = place()
    grp = lax.axis_index("grp")
    sib = seq + 1 - 2 * core
    quarter = seq % 4
    clip = seq // 4
    barrier = pltpu.get_barrier_semaphore()
    greet(sib)
    greet(4 * clip + (quarter + 2) % 4 + 1 - 2 * core)

    def greet_one(i, carry):
        greet(2 * ((chip + i) % 16) + core)
        return carry

    lax.fori_loop(1, 16, greet_one, 0)
    for j in range(1, 4):
        greet((grp + j) % 4, "grp")
    enc[z, y, core] = enc_in[...]
    merge[...] = head_merge(32 * quarter)
    ctxf[...] = jnp.zeros_like(ctxf)
    kv_out[:, :, EP:LANE, :] = jnp.zeros((16, 2, LANE - EP, KEYS), BF)
    pl.semaphore_wait(barrier, 20)

    gather = Gather(enc, ag_send, ag_recv)
    gather.start()

    def cross_x(j):
        mine = ctx4.at[grp]
        return remote(mine, mine, x_send.at[j - 1], x_recv.at[j - 1], (grp + j) % 4, "grp")

    def send_ctx(i):
        to = (chip + i) % 16
        return remote(
            sel.at[to // 2],
            kv_out.at[chip, core, pl.ds(0, EP)],
            c_send.at[i],
            c_recv.at[i],
            2 * to + core,
        )

    own_ctx = pltpu.make_async_copy(
        sel.at[clip], kv_out.at[chip, core, pl.ds(0, EP)], c_send.at[0]
    )
    half = kv_out.at[:, core, pl.ds(0, EP)]
    share = remote(half, half, p_send, p_recv, sib)

    def send_win(j):
        return remote(
            outw.at[j],
            win_out.at[quarter],
            q_send.at[j],
            q_recv.at[j],
            4 * clip + (quarter + j) % 4,
        )

    own_win = pltpu.make_async_copy(outw.at[0], win_out.at[quarter], q_send.at[0])

    def make_context():
        gather.finish()

        def one(n, carry):
            at = pl.multiple_of(n * 512, 512)
            left = enc[:, :, :, :, pl.ds(at, 512)].reshape(KEYS, 512)
            ctxf[:, 0:E] += jnp.dot(left, wkv[pl.ds(at, 512), :], preferred_element_type=F32)
            return carry

        lax.fori_loop(0, 8, one, 0)
        turned = jnp.transpose(ctxf[...])[0:EP, :]
        row = lax.broadcasted_iota(jnp.int32, (EP, KEYS), 0)
        ctx4[grp] = jnp.where(row == E, 1.0, turned).astype(BF)
        for j in range(1, 4):
            cross_x(j).start()

    def spread_context():
        for j in range(1, 4):
            cross_x(j).wait_recv()

        def choose(c, carry):
            def look(i, found):
                return jnp.where(clip_order[i] == grp * 8 + c, i, found)

            caption = lax.fori_loop(0, 32, look, jnp.int32(0))
            sel[c] = ctx4[caption // 8]
            return carry

        lax.fori_loop(0, 8, choose, 0)
        own_ctx.start()

        def one(i, carry):
            send_ctx(i).start()
            return carry

        lax.fori_loop(1, 16, one, 0)

    def share_context():
        own_ctx.wait()

        def one(i, carry):
            send_ctx(i).wait_recv()
            return carry

        lax.fori_loop(1, 16, one, 0)
        share.start()

    def attend(step, carry):
        j = (step // 2 + 1) % 4
        half_at = step % 2
        at = 4 * ((quarter + j) % 4) + 2 * half_at
        for h in range(4):
            query = heads[0, h, pl.ds(at, 2)].reshape(256, LANE)
            key_rows = heads[1, h].reshape(VT, LANE)
            value_rows = heads[2, h].reshape(VT, LANE)
            score = lax.dot_general(
                query, key_rows, (((1,), (1,)), ((), ())), preferred_element_type=F32
            )
            weight = jnp.exp2(score - jnp.max(score, axis=-1, keepdims=True)).astype(BF)
            value = jnp.dot(weight, value_rows, preferred_element_type=F32)
            value = value / value[:, E : E + 1]
            mix[:, h * LANE : (h + 1) * LANE] = value.astype(BF)
        outw[j, pl.ds(pl.multiple_of(256 * half_at, 256), 256)] = jnp.dot(
            mix[...], merge[...], preferred_element_type=F32
        ).astype(BF)

        @pl.when((half_at == 1) & (j > 0))
        def _():
            send_win(j).start()

        @pl.when(step == 0)
        def _():
            gather.middle()

        @pl.when(step == 2)
        def _():
            gather.last()

        @pl.when(step == 3)
        def _():
            make_context()

        @pl.when(step == 4)
        def _():
            spread_context()

        @pl.when(step == 6)
        def _():
            share_context()

        return carry

    lax.fori_loop(0, 8, attend, 0)
    own_win.start()
    own_win.wait()
    for j in range(1, 4):
        send_win(j).wait()
        cross_x(j).wait_send()
    share.wait()

    def drain(i, carry):
        send_ctx(i).wait_send()
        return carry

    lax.fori_loop(1, 16, drain, 0)


def cross_kernel(
    clip_order,
    lengths,
    mod,
    win,
    kv,
    residual,
    wo,
    wcq,
    wco,
    out,
    select,
    merge,
    query,
    heads,
    hidden,
    crossw,
    done,
    s_sem,
    r_sem,
):
    seq, core, chip, y, z = place()
    grp = lax.axis_index("grp")
    quarter = seq % 4
    clip = seq // 4
    barrier = pltpu.get_barrier_semaphore()
    own_here = z == quarter

    def greet_one(i, carry):
        @pl.when(4 * i + z != seq)
        def _():
            greet(4 * i + z)

        return carry

    lax.fori_loop(0, 8, greet_one, 0)
    for n in range(4):
        select[n] = head_select(32 * n)
        merge[n] = head_merge(32 * n)

    def look(i, found):
        return jnp.where(clip_order[i] == grp * 8 + clip, i, found)

    caption = lax.fori_loop(0, 32, look, jnp.int32(0))
    pack = caption // 8
    item = caption % 8
    begin = jnp.int32(0)
    finish = jnp.int32(0)
    for n in range(8):
        size = lengths[pack, n]
        begin = begin + jnp.where(n < item, size, 0)
        finish = finish + jnp.where(n <= item, size, 0)
    gate = mod[clip, 2:3, :]
    pl.semaphore_wait(barrier, jnp.where(own_here, 7, 8))

    def send(b):
        return remote(done.at[b], out.at[clip], s_sem.at[b], r_sem.at[clip], 8 * quarter + b)

    def send_own(b):
        return pltpu.make_async_copy(done.at[b], out.at[clip], s_sem.at[b])

    def rows(n, carry):
        at = pl.multiple_of(256 * n, 256)
        update = jnp.dot(win[0, pl.ds(at, 256)], wo[0:WIN, :], preferred_element_type=F32)
        for i in range(1, 4):
            update = update + jnp.dot(
                win[i, pl.ds(at, 256)], wo[256 * i : 256 * i + WIN, :], preferred_element_type=F32
            )
        base = residual[pl.ds(4 * n, 4)].reshape(256, D).astype(F32)
        hidden[...] = (base + gate * update).astype(BF)
        query[...] = (
            jnp.dot(hidden[...], wcq[...], preferred_element_type=F32) * QSCALE
        ).astype(BF)
        key_at = lax.broadcasted_iota(jnp.int32, (256, KEYS), 1)
        keep = (key_at >= begin) & (key_at < finish)
        for i in range(4):
            heads[i] = jnp.dot(
                query[:, 256 * i : 256 * i + WIN], select[i], preferred_element_type=F32
            ).astype(BF)

        def four(i, carry):
            for h in range(4):
                at_head = 4 * i + h
                key_t = kv[at_head // 2, h % 2]
                value_t = kv[8 + at_head // 2, h % 2]
                score = jnp.dot(
                    heads[i, :, h * LANE : (h + 1) * LANE], key_t, preferred_element_type=F32
                )
                score = jnp.where(keep, score, -1e30)
                weight = jnp.exp2(score - jnp.max(score, axis=-1, keepdims=True)).astype(BF)
                value = lax.dot_general(
                    weight, value_t, (((1,), (1,)), ((), ())), preferred_element_type=F32
                )
                value = value / value[:, E : E + 1]
                crossw[i, :, h * LANE : (h + 1) * LANE] = value.astype(BF)
            return carry

        lax.fori_loop(0, 4, four, 0)
        total = hidden[...].astype(F32)
        for i in range(4):
            window = jnp.dot(crossw[i], merge[i], preferred_element_type=F32).astype(BF)
            total = total + jnp.dot(
                window, wco[256 * i : 256 * i + WIN, :], preferred_element_type=F32
            )
        done[pl.ds(4 * n, 4)] = total.astype(BF).reshape(4, 64, D)
        for i in range(4):
            b = 4 * n + i

            @pl.when(8 * quarter + b == seq)
            def _():
                send_own(b).start()

            @pl.when(8 * quarter + b != seq)
            def _():
                send(b).start()

        return carry

    lax.fori_loop(0, 2, rows, 0)

    def drain(b, carry):
        @pl.when(8 * quarter + b == seq)
        def _():
            send_own(b).wait()

        @pl.when(8 * quarter + b != seq)
        def _():
            send(b).wait_send()

        @pl.when(4 * b + z != seq)
        def _():
            pltpu.make_async_remote_copy(
                src_ref=done.at[0],
                dst_ref=out.at[b],
                send_sem=s_sem.at[0],
                recv_sem=r_sem.at[b],
                device_id={"seq": 4 * b + z},
                device_id_type=MESH,
            ).wait_recv()

        return carry

    lax.fori_loop(0, 8, drain, 0)


def params(number):
    return pltpu.CompilerParams(
        collective_id=number, has_side_effects=True, vmem_limit_bytes=58 * MIB
    )


def per_device(
    captions,
    lengths,
    clip_order,
    t5_gain,
    w_tq,
    w_tk,
    w_tv,
    w_to,
    w_kv,
    video,
    modulation,
    w_qkv,
    w_o,
    w_cq,
    w_co,
):
    vmem = pl.BlockSpec(memory_space=pltpu.VMEM)
    smem = pl.BlockSpec(memory_space=pltpu.SMEM)
    anywhere = pl.BlockSpec(memory_space=pl.ANY)
    dma = pltpu.SemaphoreType.DMA
    heads, quarter_rows, encoded = pl.pallas_call(
        front_kernel,
        out_shape=(
            jax.ShapeDtypeStruct((3, 4, 16, 128, LANE), BF),
            jax.ShapeDtypeStruct((8, 64, D), BF),
            jax.ShapeDtypeStruct((16, DT), BF),
        ),
        in_specs=[smem, vmem, vmem, vmem] + [anywhere] * 6,
        out_specs=(vmem, anywhere, vmem),
        scratch_shapes=[
            pltpu.VMEM((4, 4, 2, 16, DT), BF),
            pltpu.VMEM((DT, 384), BF),
            pltpu.VMEM((128, DT), BF),
            pltpu.VMEM((3, D, WIN), BF),
            pltpu.VMEM((D, 3 * HP), BF),
            pltpu.VMEM((32, 64, D), BF),
            pltpu.VMEM((KEYS, 384), F32),
            pltpu.VMEM((4, 4, 2, 16, LANE), BF),
            pltpu.VMEM((4, 4, 16, DT), BF),
            pltpu.VMEM((4, 4, 16, DT), BF),
            pltpu.VMEM((4, 4, 16, DT), F32),
            pltpu.VMEM((4, 4, 16, DT), BF),
            pltpu.VMEM((2, 3, 4, 16, HALF), BF),
            pltpu.VMEM((2, 4, 16, HALF), F32),
            pltpu.VMEM((2, 4, 16, HALF), BF),
            pltpu.VMEM((2, 3, 16, HALF), BF),
            dma((8,)),
            dma((13,)),
            dma((13,)),
            dma((16,)),
            dma((16,)),
            dma((16,)),
            dma((16,)),
            dma((13,)),
            dma((13,)),
            dma,
        ],
        compiler_params=params(0),
        name="front",
    )(
        lengths,
        t5_gain.reshape(1, DT),
        captions,
        modulation,
        video,
        w_tq,
        w_tk,
        w_tv,
        w_to,
        w_qkv,
    )
    win, kv = pl.pallas_call(
        attend_kernel,
        out_shape=(
            jax.ShapeDtypeStruct((4, 512, WIN), BF),
            jax.ShapeDtypeStruct((16, 2, LANE, KEYS), BF),
        ),
        in_specs=[smem, vmem, vmem, vmem],
        out_specs=(vmem, vmem),
        scratch_shapes=[
            pltpu.VMEM((4, 4, 2, 16, DT), BF),
            pltpu.VMEM((256, HP), BF),
            pltpu.VMEM((HP, WIN), BF),
            pltpu.VMEM((4, 512, WIN), BF),
            pltpu.VMEM((KEYS, LANE), F32),
            pltpu.VMEM((4, EP, KEYS), BF),
            pltpu.VMEM((8, EP, KEYS), BF),
            dma((13,)),
            dma((13,)),
            dma((3,)),
            dma((3,)),
            dma((16,)),
            dma((16,)),
            dma,
            dma,
            dma((4,)),
            dma((4,)),
        ],
        compiler_params=params(1),
        name="attend",
    )(clip_order, encoded, w_kv, heads)
    return pl.pallas_call(
        cross_kernel,
        out_shape=jax.ShapeDtypeStruct((8, 64, D), BF),
        in_specs=[smem, smem] + [vmem] * 7,
        out_specs=anywhere,
        scratch_shapes=[
            pltpu.VMEM((4, WIN, HP), BF),
            pltpu.VMEM((4, HP, WIN), BF),
            pltpu.VMEM((256, D), BF),
            pltpu.VMEM((4, 256, HP), BF),
            pltpu.VMEM((256, D), BF),
            pltpu.VMEM((4, 256, HP), BF),
            pltpu.VMEM((8, 64, D), BF),
            dma((8,)),
            dma((8,)),
        ],
        compiler_params=params(2),
        name="cross",
    )(clip_order, lengths, modulation, win, kv, quarter_rows, w_o, w_cq, w_co)


def solution(mesh):
    in_specs = (
        P(("grp", "seq"), None),
        P(),
        P(),
        P(),
        P(None, "seq"),
        P(None, "seq"),
        P(None, "seq"),
        P("seq", None),
        P(None, "seq"),
        P("grp", "seq", None),
        P("grp", None, None),
        P(),
        P(),
        P(),
        P(),
    )
    out_specs = P("grp", "seq", None)
    return jax.shard_map(
        per_device, mesh=mesh, in_specs=in_specs, out_specs=out_specs, check_vma=False
    )
```

time: 1360 us -> 201 us (0.15)
  the two profiles are of different devices: /device:TPU:2 before, /device:TPU:25 now
where the time goes in v1:
time: 201 us
  Pallas kernels  194 us (97%)
  local copies, waits for them, and re-layouts  6.16 us (3%)
    pallas_call x1, Pallas kernels, per_device(): pl.pallas_call(front_kernel, out_shape=(jax.ShapeDtypeStruct((3, 4, 16, 1...  83 us
    pallas_call x1, Pallas kernels, per_device(): pl.pallas_call(attend_kernel, out_shape=(jax.ShapeDtypeStruct((4, 512, WI...  65.9 us
    pallas_call x1, Pallas kernels, per_device(): pl.pallas_call(cross_kernel, out_shape=jax.ShapeDtypeStruct((8, 64, D), B...  45.6 us
    unnamed x3, local copies, waits for them, and re-layouts  6.16 us

profile of v1, /device:TPU:25, one launch (start us, length us, event | category | flops | bytes accessed | tf_op | source)
XLA Modules:
  0.0 200.7 jit_solution(6328429784027998216)
XLA Ops:
  0.0 1.6 copy.18.mod
  1.6 2.2 %copy.17.wkv = bf16[4096,72]{1,0:T(8,128)(2,1)} copy(bf16[4096,72]{0,1:T(8,128)(2,1)} %param.23) | data formatting | bytes 1179648 | tf_op args[8]
  3.8 83.0 %front.1 = (bf16[3,4,16,128,128]{4,3,2,1,0:T(8,128)(2,1)}, bf16[8,64,1152]{2,1,0:T(8,128)(2,1)}, bf16[16,4096]{1,0:T(8,128)(2,1)}) custom-call(s32[4,8]{1,0:T(4,128)} %lengths.3, f32[1,4096]{1,0:T(1,128)} %bitcast.1, bf16[16,4096]{1,0:T(8,128)(2,1)} %cap_in.1, f32[8,3,1152]{2,1,0:T(4,128)} %copy.18.mod, bf16[8,64,1152]{2,1,0:T(8,128)(2,1)} %video.1, ...), custom_call_target="tpu_custom_call" | custom-call | tf_op jit(solution)/shard_map/front/pallas_call | solution.py:778
  86.8 65.9 %attend.1 = (bf16[4,512,384]{2,1,0:T(8,128)(2,1)}, bf16[16,2,128,512]{3,2,1,0:T(8,128)(2,1)}) custom-call(s32[32]{0:T(128)} %clip_order.3, bf16[16,4096]{1,0:T(8,128)(2,1)} %get-tuple-element.10.enc_in, bf16[4096,72]{1,0:T(8,128)(2,1)} %copy.17.wkv, bf16[3,4,16,128,128]{4,3,2,1,0:T(8,128)(2,1)} %get-tuple-element.11.heads), custom_call_target="tpu_custom_call" | custom-call | tf_op jit(solution)/shard_map/attend/pallas_call | solution.py:829
  152.7 45.6 %cross.1 = bf16[8,64,1152]{2,1,0:T(8,128)(2,1)} custom-call(s32[32]{0:T(128)} %clip_order.3, s32[4,8]{1,0:T(4,128)} %lengths.3, f32[8,3,1152]{2,1,0:T(4,128)} %copy.18.mod, bf16[4,512,384]{2,1,0:T(8,128)(2,1)} %get-tuple-element.12.win, bf16[16,2,128,512]{3,2,1,0:T(8,128)(2,1)} %get-tuple-element.13.kv, bf16[8,64,1152]{2,1,0:T(8,128)(2,1)} %get-tuple-element.14.residual, ...), custom_call_target="tpu_custom_call" | custom-call | tf_op jit(solution)/shard_map/cross/pallas_call | solution.py:859
  198.3 2.4 %copy.20 = bf16[8,64,1152]{2,1,0:T(8,128)(2,1)} copy(bf16[8,64,1152]{2,1,0:T(8,128)(2,1)} %cross.1) | data formatting | bytes 2359296

commit v2 on v1

--- a/solution.py
+++ b/solution.py
@@ -1,4 +1,3 @@
-import functools
 import math
 
 import jax
@@ -25,6 +24,7 @@
 QSCALE = E ** (-0.5) * LOG2E
 BF = jnp.bfloat16
 F32 = jnp.float32
+ATTEND_STEPS = ((0, "middle"), (3, "last"), (4, "context"), (5, "spread"))
 MESH = pl.DeviceIdType.MESH
 
 
@@ -61,15 +61,6 @@
     return jnp.where(hit, 1.0, 0.0).astype(BF)
 
 
-def head_merge(offset):
-    row = lax.broadcasted_iota(jnp.int32, (HP, WIN), 0)
-    col = lax.broadcasted_iota(jnp.int32, (HP, WIN), 1)
-    head = row >> 7
-    lane = row & 127
-    hit = (col == offset + head * E + lane) & (lane < E)
-    return jnp.where(hit, 1.0, 0.0).astype(BF)
-
-
 class Gather:
     def __init__(self, buf, send, recv):
         seq, core, chip, y, z = place()
@@ -79,6 +70,10 @@
         row = buf.at[z, :, core, :, pl.ds(0, HALF)]
         col = buf.at[:, y, core, :, pl.ds(HALF, HALF)]
         self.a, self.b = [], []
+        self.c = [
+            remote(row, row, send.at[12], recv.at[12], sib),
+            remote(col, col, send.at[13], recv.at[13], sib),
+        ]
         for j in range(1, 4):
             py = 8 * z + 2 * ((y + j) % 4) + core
             pz = 8 * ((z + j) % 4) + 2 * y + core
@@ -87,8 +82,10 @@
             self.a.append(remote(second, second, send.at[n + 3], recv.at[n + 3], pz))
             self.b.append(remote(row, row, send.at[n + 6], recv.at[n + 6], pz))
             self.b.append(remote(col, col, send.at[n + 9], recv.at[n + 9], py))
-        half = buf.at[:, :, core]
-        self.c = remote(half, half, send.at[12], recv.at[12], sib)
+            near = buf.at[(z + 4 - j) % 4, :, core, :, pl.ds(0, HALF)]
+            side = buf.at[:, (y + 4 - j) % 4, core, :, pl.ds(HALF, HALF)]
+            self.c.append(remote(near, near, send.at[13 + j], recv.at[13 + j], sib))
+            self.c.append(remote(side, side, send.at[16 + j], recv.at[16 + j], sib))
 
     def start(self):
         for copy in self.a:
@@ -99,15 +96,18 @@
             copy.wait_recv()
         for copy in self.b:
             copy.start()
+        for copy in self.c[:2]:
+            copy.start()
 
     def last(self):
-        for copy in self.b:
+        for copy, onward in zip(self.b, self.c[2:]):
             copy.wait_recv()
-        self.c.start()
+            onward.start()
 
     def finish(self):
-        self.c.wait_recv()
-        for copy in self.a + self.b + [self.c]:
+        for copy in self.c:
+            copy.wait_recv()
+        for copy in self.a + self.b + self.c:
             copy.wait_send()
 
 
@@ -304,8 +304,8 @@
     for copy in second:
         copy.start()
 
-    shift = mod[clip, 0:1, :]
-    scale = 1.0 + mod[clip, 1:2, :]
+    shift = mod[0, pl.ds(clip, 1), :]
+    scale = 1.0 + mod[1, pl.ds(clip, 1), :]
     vlane = lax.broadcasted_iota(jnp.int32, (256, HP), 1) & 127
 
     def forward(i):
@@ -416,21 +416,36 @@
 
 
 def attend_kernel(
+    lengths,
     clip_order,
     enc_in,
+    mod,
     wkv,
     heads,
-    win_out,
-    kv_out,
+    residual_in,
+    wo,
+    wcq,
+    wco,
+    out,
     enc,
     mix,
-    merge,
     outw,
-    ctxf,
+    win,
     ctx4,
     sel,
-    ag_send,
-    ag_recv,
+    kv,
+    select,
+    query,
+    done,
+    cross,
+    hidden,
+    residual,
+    wob,
+    wcqb,
+    wcob,
+    w_sem,
+    h_send,
+    h_recv,
     x_send,
     x_recv,
     c_send,
@@ -439,6 +454,8 @@
     p_recv,
     q_send,
     q_recv,
+    o_send,
+    o_recv,
 ):
     seq, core, chip, y, z = place()
     grp = lax.axis_index("grp")
@@ -446,24 +463,34 @@
     quarter = seq % 4
     clip = seq // 4
     barrier = pltpu.get_barrier_semaphore()
-    greet(sib)
-    greet(4 * clip + (quarter + 2) % 4 + 1 - 2 * core)
 
     def greet_one(i, carry):
-        greet(2 * ((chip + i) % 16) + core)
-        return carry
-
-    lax.fori_loop(1, 16, greet_one, 0)
+        greet((seq + i) % 32)
+        return carry
+
+    lax.fori_loop(1, 32, greet_one, 0)
     for j in range(1, 4):
         greet((grp + j) % 4, "grp")
     enc[z, y, core] = enc_in[...]
-    merge[...] = head_merge(32 * quarter)
-    ctxf[...] = jnp.zeros_like(ctxf)
-    kv_out[:, :, EP:LANE, :] = jnp.zeros((16, 2, LANE - EP, KEYS), BF)
-    pl.semaphore_wait(barrier, 20)
-
-    gather = Gather(enc, ag_send, ag_recv)
-    gather.start()
+    kv[:, :, EP:LANE, :] = jnp.zeros((16, 2, LANE - EP, KEYS), BF)
+    pl.semaphore_wait(barrier, 34)
+    again = Gather(enc, h_send, h_recv)
+    again.start()
+    loads = [
+        pltpu.make_async_copy(wo.at[:, pl.ds(n * WIN, WIN)], wob.at[n], w_sem.at[n])
+        for n in range(3)
+    ]
+    for n in range(3):
+        loads.append(
+            pltpu.make_async_copy(wcq.at[:, pl.ds(n * WIN, WIN)], wcqb.at[n], w_sem.at[3 + n])
+        )
+    loads.append(pltpu.make_async_copy(wco, wcob, w_sem.at[6]))
+    loads.append(pltpu.make_async_copy(residual_in, residual, w_sem.at[7]))
+    for copy in loads:
+        copy.start()
+    for n in range(4):
+        select[n] = head_select(32 * n)
+    gate = mod[2, pl.ds(clip, 1), :]
 
     def cross_x(j):
         mine = ctx4.at[grp]
@@ -473,42 +500,33 @@
         to = (chip + i) % 16
         return remote(
             sel.at[to // 2],
-            kv_out.at[chip, core, pl.ds(0, EP)],
+            kv.at[chip, core, pl.ds(0, EP)],
             c_send.at[i],
             c_recv.at[i],
             2 * to + core,
         )
 
-    own_ctx = pltpu.make_async_copy(
-        sel.at[clip], kv_out.at[chip, core, pl.ds(0, EP)], c_send.at[0]
-    )
-    half = kv_out.at[:, core, pl.ds(0, EP)]
+    own_ctx = pltpu.make_async_copy(sel.at[clip], kv.at[chip, core, pl.ds(0, EP)], c_send.at[0])
+    half = kv.at[:, core, pl.ds(0, EP)]
     share = remote(half, half, p_send, p_recv, sib)
 
-    def send_win(j):
-        return remote(
-            outw.at[j],
-            win_out.at[quarter],
-            q_send.at[j],
-            q_recv.at[j],
-            4 * clip + (quarter + j) % 4,
-        )
-
-    own_win = pltpu.make_async_copy(outw.at[0], win_out.at[quarter], q_send.at[0])
-
     def make_context():
-        gather.finish()
-
-        def one(n, carry):
+        again.finish()
+
+        def one(n, total):
             at = pl.multiple_of(n * 512, 512)
             left = enc[:, :, :, :, pl.ds(at, 512)].reshape(KEYS, 512)
-            ctxf[:, 0:E] += jnp.dot(left, wkv[pl.ds(at, 512), :], preferred_element_type=F32)
-            return carry
-
-        lax.fori_loop(0, 8, one, 0)
-        turned = jnp.transpose(ctxf[...])[0:EP, :]
-        row = lax.broadcasted_iota(jnp.int32, (EP, KEYS), 0)
-        ctx4[grp] = jnp.where(row == E, 1.0, turned).astype(BF)
+            return total + lax.dot_general(
+                wkv[:, pl.ds(at, 512)],
+                left,
+                (((1,), (1,)), ((), ())),
+                preferred_element_type=F32,
+            )
+
+        turned = lax.fori_loop(0, 8, one, jnp.zeros((E, KEYS), F32))
+        tail = lax.broadcasted_iota(jnp.int32, (EP - E, KEYS), 0)
+        tail = jnp.where(tail == 0, 1.0, 0.0)
+        ctx4[grp] = jnp.concatenate([turned, tail], axis=0).astype(BF)
         for j in range(1, 4):
             cross_x(j).start()
 
@@ -543,105 +561,57 @@
         lax.fori_loop(1, 16, one, 0)
         share.start()
 
+    def at_step(step, when, work):
+        @pl.when(step == when)
+        def _():
+            work()
+
+    locals_of = {
+        "middle": again.middle,
+        "last": again.last,
+        "context": make_context,
+        "spread": spread_context,
+    }
+
+    def send_win(j):
+        to = 4 * clip + (quarter + j) % 4
+        return remote(outw.at[j], win.at[quarter], q_send.at[j], q_recv.at[j], to)
+
+    own_win = pltpu.make_async_copy(outw.at[0], win.at[quarter], q_send.at[0])
+
     def attend(step, carry):
         j = (step // 2 + 1) % 4
-        half_at = step % 2
-        at = 4 * ((quarter + j) % 4) + 2 * half_at
-        for h in range(4):
-            query = heads[0, h, pl.ds(at, 2)].reshape(256, LANE)
+        at = 4 * ((quarter + j) % 4)
+        for u in range(2):
+            h = 2 * (step % 2) + u
+            q_rows = heads[0, h, pl.ds(at, 4)].reshape(512, LANE)
             key_rows = heads[1, h].reshape(VT, LANE)
             value_rows = heads[2, h].reshape(VT, LANE)
             score = lax.dot_general(
-                query, key_rows, (((1,), (1,)), ((), ())), preferred_element_type=F32
+                q_rows, key_rows, (((1,), (1,)), ((), ())), preferred_element_type=F32
             )
             weight = jnp.exp2(score - jnp.max(score, axis=-1, keepdims=True)).astype(BF)
             value = jnp.dot(weight, value_rows, preferred_element_type=F32)
             value = value / value[:, E : E + 1]
-            mix[:, h * LANE : (h + 1) * LANE] = value.astype(BF)
-        outw[j, pl.ds(pl.multiple_of(256 * half_at, 256), 256)] = jnp.dot(
-            mix[...], merge[...], preferred_element_type=F32
-        ).astype(BF)
-
-        @pl.when((half_at == 1) & (j > 0))
+            mix[h] = value.astype(BF)
+
+        @pl.when(step % 2 == 1)
+        def _():
+            flat = jnp.concatenate([mix[h] for h in range(4)], axis=1)
+            outw[j] = lax.dot_general(
+                flat, select[quarter], (((1,), (1,)), ((), ())), preferred_element_type=F32
+            ).astype(BF)
+
+        @pl.when((step % 2 == 1) & (j > 0))
         def _():
             send_win(j).start()
 
-        @pl.when(step == 0)
-        def _():
-            gather.middle()
-
-        @pl.when(step == 2)
-        def _():
-            gather.last()
-
-        @pl.when(step == 3)
-        def _():
-            make_context()
-
-        @pl.when(step == 4)
-        def _():
-            spread_context()
-
-        @pl.when(step == 6)
-        def _():
-            share_context()
-
+        for when, work in ATTEND_STEPS:
+            at_step(step, when, locals_of[work])
         return carry
 
     lax.fori_loop(0, 8, attend, 0)
     own_win.start()
-    own_win.wait()
-    for j in range(1, 4):
-        send_win(j).wait()
-        cross_x(j).wait_send()
-    share.wait()
-
-    def drain(i, carry):
-        send_ctx(i).wait_send()
-        return carry
-
-    lax.fori_loop(1, 16, drain, 0)
-
-
-def cross_kernel(
-    clip_order,
-    lengths,
-    mod,
-    win,
-    kv,
-    residual,
-    wo,
-    wcq,
-    wco,
-    out,
-    select,
-    merge,
-    query,
-    heads,
-    hidden,
-    crossw,
-    done,
-    s_sem,
-    r_sem,
-):
-    seq, core, chip, y, z = place()
-    grp = lax.axis_index("grp")
-    quarter = seq % 4
-    clip = seq // 4
-    barrier = pltpu.get_barrier_semaphore()
-    own_here = z == quarter
-
-    def greet_one(i, carry):
-        @pl.when(4 * i + z != seq)
-        def _():
-            greet(4 * i + z)
-
-        return carry
-
-    lax.fori_loop(0, 8, greet_one, 0)
-    for n in range(4):
-        select[n] = head_select(32 * n)
-        merge[n] = head_merge(32 * n)
 
     def look(i, found):
         return jnp.where(clip_order[i] == grp * 8 + clip, i, found)
@@ -655,57 +625,92 @@
         size = lengths[pack, n]
         begin = begin + jnp.where(n < item, size, 0)
         finish = finish + jnp.where(n <= item, size, 0)
-    gate = mod[clip, 2:3, :]
-    pl.semaphore_wait(barrier, jnp.where(own_here, 7, 8))
+    for copy in loads:
+        copy.wait()
+    own_win.wait()
+    for j in range(1, 4):
+        send_win(j).wait()
+
+    def before(n, carry):
+        at = pl.multiple_of(256 * n, 256)
+        for c in range(3):
+            cols = slice(c * WIN, (c + 1) * WIN)
+            update = jnp.dot(
+                win[0, pl.ds(at, 256)], wob[c, 0:WIN], preferred_element_type=F32
+            )
+            for i in range(1, 4):
+                update = update + jnp.dot(
+                    win[i, pl.ds(at, 256)],
+                    wob[c, 256 * i : 256 * i + WIN],
+                    preferred_element_type=F32,
+                )
+            first_rows = residual[pl.ds(4 * n, 4), :, cols].reshape(256, WIN)
+            hidden[pl.ds(at, 256), cols] = (
+                first_rows.astype(F32) + gate[:, cols] * update
+            ).astype(BF)
+        for c in range(3):
+            value = jnp.dot(
+                hidden[pl.ds(at, 256)], wcqb[c], preferred_element_type=F32
+            )
+            query[pl.ds(4 * n, 4), :, c * WIN : (c + 1) * WIN] = (
+                (value * QSCALE).astype(BF).reshape(4, 64, WIN)
+            )
+        for i in range(4):
+            cross[i, pl.ds(at, 256)] = jnp.dot(
+                query[pl.ds(4 * n, 4), :, 256 * i : 256 * i + WIN].reshape(256, WIN),
+                select[i],
+                preferred_element_type=F32,
+            ).astype(BF)
+        return carry
+
+    lax.fori_loop(0, 2, before, 0)
+    share_context()
+    share.wait()
 
     def send(b):
-        return remote(done.at[b], out.at[clip], s_sem.at[b], r_sem.at[clip], 8 * quarter + b)
+        return remote(done.at[b], out.at[clip], o_send.at[b], o_recv.at[clip], 8 * quarter + b)
 
     def send_own(b):
-        return pltpu.make_async_copy(done.at[b], out.at[clip], s_sem.at[b])
-
-    def rows(n, carry):
+        return pltpu.make_async_copy(done.at[b], out.at[clip], o_send.at[b])
+
+    key_at = lax.broadcasted_iota(jnp.int32, (256, KEYS), 1)
+    keep = (key_at >= begin) & (key_at < finish)
+
+    def after(n, carry):
         at = pl.multiple_of(256 * n, 256)
-        update = jnp.dot(win[0, pl.ds(at, 256)], wo[0:WIN, :], preferred_element_type=F32)
-        for i in range(1, 4):
-            update = update + jnp.dot(
-                win[i, pl.ds(at, 256)], wo[256 * i : 256 * i + WIN, :], preferred_element_type=F32
-            )
-        base = residual[pl.ds(4 * n, 4)].reshape(256, D).astype(F32)
-        hidden[...] = (base + gate * update).astype(BF)
-        query[...] = (
-            jnp.dot(hidden[...], wcq[...], preferred_element_type=F32) * QSCALE
-        ).astype(BF)
-        key_at = lax.broadcasted_iota(jnp.int32, (256, KEYS), 1)
-        keep = (key_at >= begin) & (key_at < finish)
-        for i in range(4):
-            heads[i] = jnp.dot(
-                query[:, 256 * i : 256 * i + WIN], select[i], preferred_element_type=F32
-            ).astype(BF)
 
         def four(i, carry):
             for h in range(4):
-                at_head = 4 * i + h
-                key_t = kv[at_head // 2, h % 2]
-                value_t = kv[8 + at_head // 2, h % 2]
+                at_head = 2 * i + h // 2
+                lanes = slice(h * LANE, (h + 1) * LANE)
                 score = jnp.dot(
-                    heads[i, :, h * LANE : (h + 1) * LANE], key_t, preferred_element_type=F32
+                    cross[i, pl.ds(at, 256), lanes],
+                    kv[at_head, h % 2],
+                    preferred_element_type=F32,
                 )
                 score = jnp.where(keep, score, -1e30)
                 weight = jnp.exp2(score - jnp.max(score, axis=-1, keepdims=True)).astype(BF)
                 value = lax.dot_general(
-                    weight, value_t, (((1,), (1,)), ((), ())), preferred_element_type=F32
+                    weight,
+                    kv[8 + at_head, h % 2],
+                    (((1,), (1,)), ((), ())),
+                    preferred_element_type=F32,
                 )
                 value = value / value[:, E : E + 1]
-                crossw[i, :, h * LANE : (h + 1) * LANE] = value.astype(BF)
+                cross[i, pl.ds(at, 256), lanes] = value.astype(BF)
             return carry
 
         lax.fori_loop(0, 4, four, 0)
-        total = hidden[...].astype(F32)
+        total = hidden[pl.ds(at, 256)].astype(F32)
         for i in range(4):
-            window = jnp.dot(crossw[i], merge[i], preferred_element_type=F32).astype(BF)
+            window = lax.dot_general(
+                cross[i, pl.ds(at, 256)],
+                select[i],
+                (((1,), (1,)), ((), ())),
+                preferred_element_type=F32,
+            ).astype(BF)
             total = total + jnp.dot(
-                window, wco[256 * i : 256 * i + WIN, :], preferred_element_type=F32
+                window, wcob[256 * i : 256 * i + WIN], preferred_element_type=F32
             )
         done[pl.ds(4 * n, 4)] = total.astype(BF).reshape(4, 64, D)
         for i in range(4):
@@ -721,9 +726,18 @@
 
         return carry
 
-    lax.fori_loop(0, 2, rows, 0)
-
-    def drain(b, carry):
+    lax.fori_loop(0, 2, after, 0)
+
+    for j in range(1, 4):
+        cross_x(j).wait_send()
+
+    def drain(i, carry):
+        send_ctx(i).wait_send()
+        return carry
+
+    lax.fori_loop(1, 16, drain, 0)
+
+    def drain_out(b, carry):
         @pl.when(8 * quarter + b == seq)
         def _():
             send_own(b).wait()
@@ -734,18 +748,11 @@
 
         @pl.when(4 * b + z != seq)
         def _():
-            pltpu.make_async_remote_copy(
-                src_ref=done.at[0],
-                dst_ref=out.at[b],
-                send_sem=s_sem.at[0],
-                recv_sem=r_sem.at[b],
-                device_id={"seq": 4 * b + z},
-                device_id_type=MESH,
-            ).wait_recv()
-
-        return carry
-
-    lax.fori_loop(0, 8, drain, 0)
+            remote(done.at[0], out.at[b], o_send.at[0], o_recv.at[b], 4 * b + z).wait_recv()
+
+        return carry
+
+    lax.fori_loop(0, 8, drain_out, 0)
 
 
 def params(number):
@@ -775,6 +782,7 @@
     smem = pl.BlockSpec(memory_space=pltpu.SMEM)
     anywhere = pl.BlockSpec(memory_space=pl.ANY)
     dma = pltpu.SemaphoreType.DMA
+    mods = jnp.transpose(modulation, (1, 0, 2))
     heads, quarter_rows, encoded = pl.pallas_call(
         front_kernel,
         out_shape=(
@@ -802,8 +810,8 @@
             pltpu.VMEM((2, 4, 16, HALF), BF),
             pltpu.VMEM((2, 3, 16, HALF), BF),
             dma((8,)),
-            dma((13,)),
-            dma((13,)),
+            dma((20,)),
+            dma((20,)),
             dma((16,)),
             dma((16,)),
             dma((16,)),
@@ -818,7 +826,7 @@
         lengths,
         t5_gain.reshape(1, DT),
         captions,
-        modulation,
+        mods,
         video,
         w_tq,
         w_tk,
@@ -826,55 +834,45 @@
         w_to,
         w_qkv,
     )
-    win, kv = pl.pallas_call(
+    counts = (8, 20, 20, 3, 3, 16, 16, 0, 0, 4, 4, 8, 8)
+    return pl.pallas_call(
         attend_kernel,
-        out_shape=(
-            jax.ShapeDtypeStruct((4, 512, WIN), BF),
-            jax.ShapeDtypeStruct((16, 2, LANE, KEYS), BF),
-        ),
-        in_specs=[smem, vmem, vmem, vmem],
-        out_specs=(vmem, vmem),
+        out_shape=jax.ShapeDtypeStruct((8, 64, D), BF),
+        in_specs=[smem, smem, vmem, vmem, vmem, vmem] + [anywhere] * 4,
+        out_specs=anywhere,
         scratch_shapes=[
             pltpu.VMEM((4, 4, 2, 16, DT), BF),
-            pltpu.VMEM((256, HP), BF),
-            pltpu.VMEM((HP, WIN), BF),
+            pltpu.VMEM((4, 512, LANE), BF),
             pltpu.VMEM((4, 512, WIN), BF),
-            pltpu.VMEM((KEYS, LANE), F32),
+            pltpu.VMEM((4, 512, WIN), BF),
             pltpu.VMEM((4, EP, KEYS), BF),
             pltpu.VMEM((8, EP, KEYS), BF),
-            dma((13,)),
-            dma((13,)),
-            dma((3,)),
-            dma((3,)),
-            dma((16,)),
-            dma((16,)),
-            dma,
-            dma,
-            dma((4,)),
-            dma((4,)),
-        ],
+            pltpu.VMEM((16, 2, LANE, KEYS), BF),
+            pltpu.VMEM((4, WIN, HP), BF),
+            pltpu.VMEM((8, 64, D), BF),
+            pltpu.VMEM((8, 64, D), BF),
+            pltpu.VMEM((4, 512, HP), BF),
+            pltpu.VMEM((512, D), BF),
+            pltpu.VMEM((8, 64, D), BF),
+            pltpu.VMEM((3, D, WIN), BF),
+            pltpu.VMEM((3, D, WIN), BF),
+            pltpu.VMEM((D, D), BF),
+        ]
+        + [dma((n,)) if n else dma for n in counts],
         compiler_params=params(1),
         name="attend",
-    )(clip_order, encoded, w_kv, heads)
-    return pl.pallas_call(
-        cross_kernel,
-        out_shape=jax.ShapeDtypeStruct((8, 64, D), BF),
-        in_specs=[smem, smem] + [vmem] * 7,
-        out_specs=anywhere,
-        scratch_shapes=[
-            pltpu.VMEM((4, WIN, HP), BF),
-            pltpu.VMEM((4, HP, WIN), BF),
-            pltpu.VMEM((256, D), BF),
-            pltpu.VMEM((4, 256, HP), BF),
-            pltpu.VMEM((256, D), BF),
-            pltpu.VMEM((4, 256, HP), BF),
-            pltpu.VMEM((8, 64, D), BF),
-            dma((8,)),
-            dma((8,)),
-        ],
-        compiler_params=params(2),
-        name="cross",
-    )(clip_order, lengths, modulation, win, kv, quarter_rows, w_o, w_cq, w_co)
+    )(
+        lengths,
+        clip_order,
+        encoded,
+        mods,
+        w_kv.T,
+        heads,
+        quarter_rows,
+        w_o,
+        w_cq,
+        w_co,
+    )
 
 
 def solution(mesh):

time: 201 us -> 178 us (0.89)
  Pallas kernels: 194 us -> 175 us
  local copies, waits for them, and re-layouts: 6.16 us -> 2.37 us
    pallas_call x2 -> x1, Pallas kernels: 111 us -> 94 us  [per_device(): pl.pallas_call(attend_kernel, out_shape=jax.ShapeDtypeStruct((8, 64, D),...]
    unnamed x3 -> x1, local copies, waits for them, and re-layouts: 6.16 us -> 2.37 us
where the time goes in v2:
time: 178 us
  Pallas kernels  175 us (98%)
  local copies, waits for them, and re-layouts  2.37 us (1%)
    pallas_call x1, Pallas kernels, per_device(): pl.pallas_call(attend_kernel, out_shape=jax.ShapeDtypeStruct((8, 64, D),...  94 us
    pallas_call x1, Pallas kernels, per_device(): pl.pallas_call(front_kernel, out_shape=(jax.ShapeDtypeStruct((3, 4, 16, 1...  81.5 us

profile of v2, /device:TPU:25, one launch (start us, length us, event | category | flops | bytes accessed | tf_op | source)
XLA Modules:
  0.0 177.9 jit_solution(1842187569594235359)
XLA Ops:
  0.0 81.5 %front.1 = (bf16[3,4,16,128,128]{4,3,2,1,0:T(8,128)(2,1)}, bf16[8,64,1152]{2,1,0:T(8,128)(2,1)}, bf16[16,4096]{1,0:T(8,128)(2,1)}) custom-call(s32[4,8]{1,0:T(4,128)} %lengths.3, f32[1,4096]{1,0:T(1,128)} %bitcast.6, bf16[16,4096]{1,0:T(8,128)(2,1)} %cap_in.1, f32[3,8,1152]{2,1,0:T(8,128)} %bitcast.4, bf16[8,64,1152]{2,1,0:T(8,128)(2,1)} %video.1, ...), custom_call_target="tpu_custom_call" | custom-call | tf_op jit(solution)/shard_map/front/pallas_call | solution.py:786
  81.5 94.0 %attend.1 = bf16[8,64,1152]{2,1,0:T(8,128)(2,1)} custom-call(s32[4,8]{1,0:T(4,128)} %lengths.3, s32[32]{0:T(128)} %clip_order.1, bf16[16,4096]{1,0:T(8,128)(2,1)} %get-tuple-element.8.enc_in, f32[3,8,1152]{2,1,0:T(8,128)} %bitcast.5, bf16[72,4096]{1,0:T(8,128)(2,1)} %bitcast.3, bf16[3,4,16,128,128]{4,3,2,1,0:T(8,128)(2,1)} %get-tuple-element.9.heads, ...), custom_call_target="tpu_custom_call" | custom-call | tf_op jit(solution)/shard_map/attend/pallas_call | solution.py:838
  175.5 2.4 %copy.17 = bf16[8,64,1152]{2,1,0:T(8,128)(2,1)} copy(bf16[8,64,1152]{2,1,0:T(8,128)(2,1)} %attend.1) | data formatting | bytes 2359296

commit v3 on v2

--- a/solution.py
+++ b/solution.py
@@ -24,7 +24,7 @@
 QSCALE = E ** (-0.5) * LOG2E
 BF = jnp.bfloat16
 F32 = jnp.float32
-ATTEND_STEPS = ((0, "middle"), (3, "last"), (4, "context"), (5, "spread"))
+ATTEND_STEPS = ((0, "middle"), (3, "last"), (3, "context"), (4, "spread"))
 MESH = pl.DeviceIdType.MESH
 
 
@@ -125,6 +125,7 @@
     heads_out,
     quarter_out,
     enc_out,
+    heads,
     cap,
     wt,
     wto,
@@ -151,6 +152,7 @@
     r_send,
     r_recv,
     o_sem,
+    k_sem,
 ):
     seq, core, chip, y, z = place()
     grp = lax.axis_index("grp")
@@ -325,6 +327,10 @@
     forward(0).start()
     arrive(1)
 
+    def keep_heads(i):
+        at = (chip + 16 - i) % 16
+        return pltpu.make_async_copy(heads.at[:, :, at], heads_out.at[:, :, at], k_sem.at[i])
+
     def project_video(n, carry):
         @pl.when(n < 7)
         def _():
@@ -347,8 +353,10 @@
             value = value.astype(BF)
             for h in range(4):
                 piece = value[:, h * LANE : (h + 1) * LANE]
-                heads_out[which, h, at0] = piece[:128]
-                heads_out[which, h, at1] = piece[128:]
+                heads[which, h, at0] = piece[:128]
+                heads[which, h, at1] = piece[128:]
+        keep_heads(2 * n).start()
+        keep_heads(2 * n + 1).start()
         return carry
 
     lax.fori_loop(0, 8, project_video, 0)
@@ -414,6 +422,12 @@
     lax.fori_loop(1, 16, drain, 0)
     forward(0).wait_send()
 
+    def drain_heads(i, carry):
+        keep_heads(i).wait()
+        return carry
+
+    lax.fori_loop(0, 16, drain_heads, 0)
+
 
 def attend_kernel(
     lengths,
@@ -421,12 +435,13 @@
     enc_in,
     mod,
     wkv,
-    heads,
+    heads_in,
     residual_in,
     wo,
     wcq,
     wco,
     out,
+    heads,
     enc,
     mix,
     outw,
@@ -464,6 +479,9 @@
     clip = seq // 4
     barrier = pltpu.get_barrier_semaphore()
 
+    heads_load = pltpu.make_async_copy(heads_in, heads, w_sem.at[8])
+    heads_load.start()
+
     def greet_one(i, carry):
         greet((seq + i) % 32)
         return carry
@@ -473,6 +491,10 @@
         greet((grp + j) % 4, "grp")
     enc[z, y, core] = enc_in[...]
     kv[:, :, EP:LANE, :] = jnp.zeros((16, 2, LANE - EP, KEYS), BF)
+    captions = [jnp.int32(0)] * 8
+    for i in range(32):
+        which = clip_order[i] - grp * 8
+        captions = [jnp.where(which == c, i, found) for c, found in enumerate(captions)]
     pl.semaphore_wait(barrier, 34)
     again = Gather(enc, h_send, h_recv)
     again.start()
@@ -507,8 +529,10 @@
         )
 
     own_ctx = pltpu.make_async_copy(sel.at[clip], kv.at[chip, core, pl.ds(0, EP)], c_send.at[0])
-    half = kv.at[:, core, pl.ds(0, EP)]
-    share = remote(half, half, p_send, p_recv, sib)
+
+    def share(i):
+        rows = kv.at[(chip + 16 - i) % 16, core, pl.ds(0, EP)]
+        return remote(rows, rows, p_send.at[i], p_recv.at[i], sib)
 
     def make_context():
         again.finish()
@@ -534,15 +558,8 @@
         for j in range(1, 4):
             cross_x(j).wait_recv()
 
-        def choose(c, carry):
-            def look(i, found):
-                return jnp.where(clip_order[i] == grp * 8 + c, i, found)
-
-            caption = lax.fori_loop(0, 32, look, jnp.int32(0))
-            sel[c] = ctx4[caption // 8]
-            return carry
-
-        lax.fori_loop(0, 8, choose, 0)
+        for c in range(8):
+            sel[c] = ctx4[captions[c] // 8]
         own_ctx.start()
 
         def one(i, carry):
@@ -553,13 +570,20 @@
 
     def share_context():
         own_ctx.wait()
+        share(0).start()
 
         def one(i, carry):
             send_ctx(i).wait_recv()
+            share(i).start()
             return carry
 
         lax.fori_loop(1, 16, one, 0)
-        share.start()
+
+        def got(i, carry):
+            share(i).wait()
+            return carry
+
+        lax.fori_loop(0, 16, got, 0)
 
     def at_step(step, when, work):
         @pl.when(step == when)
@@ -610,13 +634,13 @@
             at_step(step, when, locals_of[work])
         return carry
 
+    heads_load.wait()
     lax.fori_loop(0, 8, attend, 0)
     own_win.start()
 
-    def look(i, found):
-        return jnp.where(clip_order[i] == grp * 8 + clip, i, found)
-
-    caption = lax.fori_loop(0, 32, look, jnp.int32(0))
+    caption = captions[0]
+    for c in range(1, 8):
+        caption = jnp.where(clip == c, captions[c], caption)
     pack = caption // 8
     item = caption % 8
     begin = jnp.int32(0)
@@ -665,7 +689,6 @@
 
     lax.fori_loop(0, 2, before, 0)
     share_context()
-    share.wait()
 
     def send(b):
         return remote(done.at[b], out.at[clip], o_send.at[b], o_recv.at[clip], 8 * quarter + b)
@@ -791,8 +814,9 @@
             jax.ShapeDtypeStruct((16, DT), BF),
         ),
         in_specs=[smem, vmem, vmem, vmem] + [anywhere] * 6,
-        out_specs=(vmem, anywhere, vmem),
+        out_specs=(anywhere, anywhere, vmem),
         scratch_shapes=[
+            pltpu.VMEM((3, 4, 16, 128, LANE), BF),
             pltpu.VMEM((4, 4, 2, 16, DT), BF),
             pltpu.VMEM((DT, 384), BF),
             pltpu.VMEM((128, DT), BF),
@@ -819,6 +843,7 @@
             dma((13,)),
             dma((13,)),
             dma,
+            dma((16,)),
         ],
         compiler_params=params(0),
         name="front",
@@ -834,13 +859,14 @@
         w_to,
         w_qkv,
     )
-    counts = (8, 20, 20, 3, 3, 16, 16, 0, 0, 4, 4, 8, 8)
+    counts = (9, 20, 20, 3, 3, 16, 16, 16, 16, 4, 4, 8, 8)
     return pl.pallas_call(
         attend_kernel,
         out_shape=jax.ShapeDtypeStruct((8, 64, D), BF),
-        in_specs=[smem, smem, vmem, vmem, vmem, vmem] + [anywhere] * 4,
+        in_specs=[smem, smem, vmem, vmem, vmem] + [anywhere] * 5,
         out_specs=anywhere,
         scratch_shapes=[
+            pltpu.VMEM((3, 4, 16, 128, LANE), BF),
             pltpu.VMEM((4, 4, 2, 16, DT), BF),
             pltpu.VMEM((4, 512, LANE), BF),
             pltpu.VMEM((4, 512, WIN), BF),

time: 178 us -> 181 us (1.017)
  Pallas kernels: 175 us -> 178 us
    pallas_call x1, Pallas kernels: 94 us -> 98.3 us  [per_device(): pl.pallas_call(attend_kernel, out_shape=jax.ShapeDtypeStruct((8, 64, D),...]
where the time goes in v3:
time: 181 us
  Pallas kernels  178 us (98%)
  local copies, waits for them, and re-layouts  2.37 us (1%)
    pallas_call x1, Pallas kernels, per_device(): pl.pallas_call(attend_kernel, out_shape=jax.ShapeDtypeStruct((8, 64, D),...  98.3 us
    pallas_call x1, Pallas kernels, per_device(): pl.pallas_call(front_kernel, out_shape=(jax.ShapeDtypeStruct((3, 4, 16, 1...  79.8 us

profile of v3, /device:TPU:25, one launch (start us, length us, event | category | flops | bytes accessed | tf_op | source)
XLA Modules:
  0.0 180.6 jit_solution(10341171638489130353)
XLA Ops:
  0.0 79.8 %front.1 = (bf16[3,4,16,128,128]{4,3,2,1,0:T(8,128)(2,1)}, bf16[8,64,1152]{2,1,0:T(8,128)(2,1)}, bf16[16,4096]{1,0:T(8,128)(2,1)}) custom-call(s32[4,8]{1,0:T(4,128)} %lengths.3, f32[1,4096]{1,0:T(1,128)} %bitcast.6, bf16[16,4096]{1,0:T(8,128)(2,1)} %cap_in.1, f32[3,8,1152]{2,1,0:T(8,128)} %bitcast.4, bf16[8,64,1152]{2,1,0:T(8,128)(2,1)} %video.1, ...), custom_call_target="tpu_custom_call" | custom-call | tf_op jit(solution)/shard_map/front/pallas_call | solution.py:809
  79.8 98.3 %attend.1 = bf16[8,64,1152]{2,1,0:T(8,128)(2,1)} custom-call(s32[4,8]{1,0:T(4,128)} %lengths.3, s32[32]{0:T(128)} %clip_order.1, bf16[16,4096]{1,0:T(8,128)(2,1)} %get-tuple-element.8.enc_in, f32[3,8,1152]{2,1,0:T(8,128)} %bitcast.5, bf16[72,4096]{1,0:T(8,128)(2,1)} %bitcast.3, bf16[3,4,16,128,128]{4,3,2,1,0:T(8,128)(2,1)} %get-tuple-element.9.heads_in, ...), custom_call_target="tpu_custom_call" | custom-call | tf_op jit(solution)/shard_map/attend/pallas_call | solution.py:863
  178.2 2.4 %copy.17 = bf16[8,64,1152]{2,1,0:T(8,128)(2,1)} copy(bf16[8,64,1152]{2,1,0:T(8,128)(2,1)} %attend.1) | data formatting | bytes 2359296

commit v4 on v3

--- a/solution.py
+++ b/solution.py
@@ -24,7 +24,7 @@
 QSCALE = E ** (-0.5) * LOG2E
 BF = jnp.bfloat16
 F32 = jnp.float32
-ATTEND_STEPS = ((0, "middle"), (3, "last"), (3, "context"), (4, "spread"))
+ATTEND_STEPS = ((0, "middle"), (3, "last"), (4, "context"), (5, "spread"))
 MESH = pl.DeviceIdType.MESH
 
 

time: 181 us -> 172 us (0.950)
  Pallas kernels: 178 us -> 170 us
    pallas_call x1, Pallas kernels: 98.3 us -> 89.8 us  [per_device(): pl.pallas_call(attend_kernel, out_shape=jax.ShapeDtypeStruct((8, 64, D),...]
where the time goes in v4:
time: 172 us
  Pallas kernels  170 us (99%)
  local copies, waits for them, and re-layouts  2.37 us (1%)
    pallas_call x1, Pallas kernels, per_device(): pl.pallas_call(attend_kernel, out_shape=jax.ShapeDtypeStruct((8, 64, D),...  89.8 us
    pallas_call x1, Pallas kernels, per_device(): pl.pallas_call(front_kernel, out_shape=(jax.ShapeDtypeStruct((3, 4, 16, 1...  79.8 us

profile of v4, /device:TPU:25, one launch (start us, length us, event | category | flops | bytes accessed | tf_op | source)
XLA Modules:
  0.0 172.1 jit_solution(4674181713605434036)
XLA Ops:
  0.0 79.8 %front.1 = (bf16[3,4,16,128,128]{4,3,2,1,0:T(8,128)(2,1)}, bf16[8,64,1152]{2,1,0:T(8,128)(2,1)}, bf16[16,4096]{1,0:T(8,128)(2,1)}) custom-call(s32[4,8]{1,0:T(4,128)} %lengths.3, f32[1,4096]{1,0:T(1,128)} %bitcast.6, bf16[16,4096]{1,0:T(8,128)(2,1)} %cap_in.1, f32[3,8,1152]{2,1,0:T(8,128)} %bitcast.4, bf16[8,64,1152]{2,1,0:T(8,128)(2,1)} %video.1, ...), custom_call_target="tpu_custom_call" | custom-call | tf_op jit(solution)/shard_map/front/pallas_call | solution.py:809
  79.8 89.8 %attend.1 = bf16[8,64,1152]{2,1,0:T(8,128)(2,1)} custom-call(s32[4,8]{1,0:T(4,128)} %lengths.3, s32[32]{0:T(128)} %clip_order.1, bf16[16,4096]{1,0:T(8,128)(2,1)} %get-tuple-element.8.enc_in, f32[3,8,1152]{2,1,0:T(8,128)} %bitcast.5, bf16[72,4096]{1,0:T(8,128)(2,1)} %bitcast.3, bf16[3,4,16,128,128]{4,3,2,1,0:T(8,128)(2,1)} %get-tuple-element.9.heads_in, ...), custom_call_target="tpu_custom_call" | custom-call | tf_op jit(solution)/shard_map/attend/pallas_call | solution.py:863
  169.7 2.4 %copy.17 = bf16[8,64,1152]{2,1,0:T(8,128)(2,1)} copy(bf16[8,64,1152]{2,1,0:T(8,128)(2,1)} %attend.1) | data formatting | bytes 2359296

commit v5 on v4

--- a/solution.py
+++ b/solution.py
@@ -194,6 +194,16 @@
     gather = Gather(cap, ag_send, ag_recv)
     gather.start()
 
+    def send_video(i):
+        to = (chip + i) % 16
+        return remote(video.at[to // 2], vid.at[seq], v_send.at[i], v_recv.at[i], 2 * to + core)
+
+    def start_video(i, carry):
+        send_video(i).start()
+        return carry
+
+    lax.fori_loop(1, 16, start_video, 0)
+
     for copy in loads[4:]:
         copy.wait()
     select = head_select(32 * quarter)
@@ -203,15 +213,6 @@
         ).astype(BF)
     gather.middle()
 
-    def send_video(i):
-        to = (chip + i) % 16
-        return remote(video.at[to // 2], vid.at[seq], v_send.at[i], v_recv.at[i], 2 * to + core)
-
-    def start_video(i, carry):
-        send_video(i).start()
-        return carry
-
-    lax.fori_loop(1, 16, start_video, 0)
     for copy in loads[:4]:
         copy.wait()
     own_video.wait()

time: 172 us -> 181 us (1.052)
  Pallas kernels: 170 us -> 178 us
    pallas_call x1, Pallas kernels: 79.8 us -> 86.5 us  [per_device(): pl.pallas_call(front_kernel, out_shape=(jax.ShapeDtypeStruct((3, 4, 16, 1...]
where the time goes in v5:
time: 181 us; the launch traced here: 180 us
  Pallas kernels  178 us (98%)
  local copies, waits for them, and re-layouts  2.37 us (1%)
    pallas_call x1, Pallas kernels, per_device(): pl.pallas_call(attend_kernel, out_shape=jax.ShapeDtypeStruct((8, 64, D),...  91.5 us
    pallas_call x1, Pallas kernels, per_device(): pl.pallas_call(front_kernel, out_shape=(jax.ShapeDtypeStruct((3, 4, 16, 1...  86.5 us

profile of v5, /device:TPU:25, one launch (start us, length us, event | category | flops | bytes accessed | tf_op | source)
XLA Modules:
  0.0 180.5 jit_solution(3554511481798570705)
XLA Ops:
  0.0 86.5 %front.1 = (bf16[3,4,16,128,128]{4,3,2,1,0:T(8,128)(2,1)}, bf16[8,64,1152]{2,1,0:T(8,128)(2,1)}, bf16[16,4096]{1,0:T(8,128)(2,1)}) custom-call(s32[4,8]{1,0:T(4,128)} %lengths.3, f32[1,4096]{1,0:T(1,128)} %bitcast.6, bf16[16,4096]{1,0:T(8,128)(2,1)} %cap_in.1, f32[3,8,1152]{2,1,0:T(8,128)} %bitcast.4, bf16[8,64,1152]{2,1,0:T(8,128)(2,1)} %video.1, ...), custom_call_target="tpu_custom_call" | custom-call | tf_op jit(solution)/shard_map/front/pallas_call | solution.py:810
  86.6 91.5 %attend.1 = bf16[8,64,1152]{2,1,0:T(8,128)(2,1)} custom-call(s32[4,8]{1,0:T(4,128)} %lengths.3, s32[32]{0:T(128)} %clip_order.1, bf16[16,4096]{1,0:T(8,128)(2,1)} %get-tuple-element.8.enc_in, f32[3,8,1152]{2,1,0:T(8,128)} %bitcast.5, bf16[72,4096]{1,0:T(8,128)(2,1)} %bitcast.3, bf16[3,4,16,128,128]{4,3,2,1,0:T(8,128)(2,1)} %get-tuple-element.9.heads_in, ...), custom_call_target="tpu_custom_call" | custom-call | tf_op jit(solution)/shard_map/attend/pallas_call | solution.py:864
  178.1 2.4 %copy.17 = bf16[8,64,1152]{2,1,0:T(8,128)(2,1)} copy(bf16[8,64,1152]{2,1,0:T(8,128)(2,1)} %attend.1) | data formatting | bytes 2359296

commit v6 on v4

--- a/solution.py
+++ b/solution.py
@@ -359,9 +359,7 @@
         keep_heads(2 * n + 1).start()
         return carry
 
-    lax.fori_loop(0, 8, project_video, 0)
-    keep = pltpu.make_async_copy(vid.at[pl.ds(8 * quarter, 8)], quarter_out, o_sem)
-    keep.start()
+    lax.fori_loop(0, 6, project_video, 0)
 
     for copy in second:
         copy.wait_recv()
@@ -399,6 +397,10 @@
         )
     for copy in third:
         copy.start()
+    lax.fori_loop(6, 8, project_video, 0)
+    keep = pltpu.make_async_copy(vid.at[pl.ds(8 * quarter, 8)], quarter_out, o_sem)
+    keep.start()
+
     for copy in third:
         copy.wait_recv()
     first = part[0, z]

time: 172 us -> 172 us (level)
  no operation moved by 1% of the time
where the time goes in v6:
time: 172 us
  Pallas kernels  170 us (99%)
  local copies, waits for them, and re-layouts  2.37 us (1%)
    pallas_call x1, Pallas kernels, per_device(): pl.pallas_call(attend_kernel, out_shape=jax.ShapeDtypeStruct((8, 64, D),...  90.7 us
    pallas_call x1, Pallas kernels, per_device(): pl.pallas_call(front_kernel, out_shape=(jax.ShapeDtypeStruct((3, 4, 16, 1...  78.9 us

profile of v6, /device:TPU:25, one launch (start us, length us, event | category | flops | bytes accessed | tf_op | source)
XLA Modules:
  0.0 172.0 jit_solution(10160696573138914727)
XLA Ops:
  0.0 78.9 %front.1 = (bf16[3,4,16,128,128]{4,3,2,1,0:T(8,128)(2,1)}, bf16[8,64,1152]{2,1,0:T(8,128)(2,1)}, bf16[16,4096]{1,0:T(8,128)(2,1)}) custom-call(s32[4,8]{1,0:T(4,128)} %lengths.3, f32[1,4096]{1,0:T(1,128)} %bitcast.6, bf16[16,4096]{1,0:T(8,128)(2,1)} %cap_in.1, f32[3,8,1152]{2,1,0:T(8,128)} %bitcast.4, bf16[8,64,1152]{2,1,0:T(8,128)(2,1)} %video.1, ...), custom_call_target="tpu_custom_call" | custom-call | tf_op jit(solution)/shard_map/front/pallas_call | solution.py:811
  78.9 90.7 %attend.1 = bf16[8,64,1152]{2,1,0:T(8,128)(2,1)} custom-call(s32[4,8]{1,0:T(4,128)} %lengths.3, s32[32]{0:T(128)} %clip_order.1, bf16[16,4096]{1,0:T(8,128)(2,1)} %get-tuple-element.8.enc_in, f32[3,8,1152]{2,1,0:T(8,128)} %bitcast.5, bf16[72,4096]{1,0:T(8,128)(2,1)} %bitcast.3, bf16[3,4,16,128,128]{4,3,2,1,0:T(8,128)(2,1)} %get-tuple-element.9.heads_in, ...), custom_call_target="tpu_custom_call" | custom-call | tf_op jit(solution)/shard_map/attend/pallas_call | solution.py:865
  169.6 2.4 %copy.17 = bf16[8,64,1152]{2,1,0:T(8,128)(2,1)} copy(bf16[8,64,1152]{2,1,0:T(8,128)(2,1)} %attend.1) | data formatting | bytes 2359296
